TPU v7x, 256 devices: a whole 4x4x8 slice. The times are simulated.
256 devices in a mesh: gx: 64 (over z, x, core), gz: 4 (over y).
Axes of the slice: x: 4, y: 4, z: 8, core: 2. Of those that a mesh axis runs over, the one named last changes fastest.
Arguments:
- fields: float32 [3, 4096, 12288], P(None, 'gx', 'gz'), may hold values from -6 to 6
- register: float32 [3, 4096, 12288], P(None, 'gx', 'gz'), may hold values from -3 to 3
- source: float32 [4096, 12288], P('gx', 'gz'), may hold values from -0.25 to 0.25
- metric: float32 [4096], P('gx'), may hold values from 0.5 to 2
- curvature: float32 [4096], P('gx'), may hold values from -12 to 12
Outputs:
- new_fields: float32 [3, 4096, 12288], P(None, 'gx', 'gz')
- new_register: float32 [3, 4096, 12288], P(None, 'gx', 'gz')
- velocity: float32 [4096, 12288], P('gx', 'gz')
All inputs are finite; a program needn't handle non-finite values. Where the computation divides by a largest or mean magnitude, that divisor is 1e-20 or more.
Results may differ from a plain program's by a relative error of at most 0.0001.
Values sent between devices are 32-bit elements; how exact they have to be, the bound alone decides.
No kernel may reach another device: no remote copies, remote signals or barrier semaphores. Data moves between devices by JAX's collectives and lax.ppermute only.
A program may use at most 64 MiB of HBM per device.

v0:
```python
import math

import jax
import jax.numpy as jnp
import numpy as np
from jax import lax
from jax.sharding import PartitionSpec as P

ALPHA_ONE = 1.0 / 3.0
COEF_ONE = 14.0 / 9.0
WIDE_ONE = 1.0 / 9.0
ALPHA_TWO = 2.0 / 11.0
COEF_TWO = 12.0 / 11.0
WIDE_TWO = 3.0 / 11.0
VISCOSITY = 0.25
DIFFUSIVITY = 0.2
COURANT = 1.2
KEEP_FACTOR = -5.0 / 9.0
STEP_FACTOR = 15.0 / 16.0


def with_halo(block, sides, width):
    for axis, dim in sides:
        count = lax.axis_size(axis)
        forward = [(i, i + 1) for i in range(count - 1)]
        backward = [(target, source) for source, target in forward]
        low = lax.ppermute(
            lax.slice_in_dim(block, block.shape[dim] - width, None, axis=dim), axis, forward
        )
        high = lax.ppermute(lax.slice_in_dim(block, 0, width, axis=dim), axis, backward)
        block = jnp.concatenate([low, block, high], axis=dim)
    return block


def shifted(value, axis, steps):
    count = lax.axis_size(axis)
    leading, last = (max(0, -steps), min(count, count - steps))
    return lax.ppermute(value, axis, [(source, source + steps) for source in range(leading, last)])


def log_sinh(values):
    return values + np.log(1.0 - np.exp(-2.0 * values)) - math.log(2.0)


def inverse_table(alpha, length):
    ratio = 0.5 / alpha
    angle_value = math.log(ratio + math.sqrt(ratio * ratio - 1.0))
    row_index = np.arange(1, length + 1) * 1.0
    smaller = np.minimum(row_index[:, None], row_index[None, :])
    larger = np.maximum(row_index[:, None], row_index[None, :])
    magnitude = (
        np.exp(
            log_sinh(smaller * angle_value)
            + log_sinh((length + 1 - larger) * angle_value)
            - log_sinh(angle_value)
            - log_sinh((length + 1) * angle_value)
        )
        / alpha
    )
    sign_table = np.where((row_index[:, None] + row_index[None, :]) % 2 == 0, 1.0, -1.0)
    return magnitude * sign_table


def first_right(padded):
    return COEF_ONE / 2.0 * (padded[:, 3:-1] - padded[:, 1:-3]) + WIDE_ONE / 4.0 * (
        padded[:, 4:] - padded[:, :-4]
    )


def second_right(padded):
    centre = padded[:, 2:-2]
    near = padded[:, 3:-1] - 2.0 * centre + padded[:, 1:-3]
    far = padded[:, 4:] - 2.0 * centre + padded[:, :-4]
    return COEF_TWO * near + WIDE_TWO / 4.0 * far


def local(fields, register, source, metric, curvature):
    group_size = lax.axis_size("gx")
    position = lax.axis_index("gx")
    cell_count = fields.shape[1]
    interior = cell_count - 1
    stretch = metric[:, None]
    curving = curvature[:, None]
    scaled_source = source / stretch
    wide_fields = with_halo(fields, (("gx", 1),), 2)
    lower_mask = jnp.asarray(np.tril(np.ones((cell_count, cell_count))), jnp.float32)
    running = jnp.dot(
        lower_mask,
        scaled_source,
        precision=lax.Precision.HIGHEST,
        preferred_element_type=jnp.float32,
    )
    totals = running[cell_count - 1 : cell_count]
    gathered = lax.all_gather(totals, "gx", axis=0, tiled=True)
    earlier = (jnp.arange(group_size) < position)[:, None]
    offset = jnp.sum(jnp.where(earlier, gathered, 0.0), axis=0, keepdims=True)
    velocity = -(offset + running - 0.5 * scaled_source)
    local_rate = jnp.max(jnp.abs(velocity) * stretch + 4.0 * VISCOSITY * stretch * stretch)
    max_rate = lax.pmax(local_rate, ("gx", "gz"))
    time_step = COURANT / max_rate
    wide_velocity = with_halo(velocity, (("gx", 0),), 2)
    first_sources = jnp.concatenate([wide_velocity[None], wide_fields], 0)
    right_one = first_right(first_sources)
    right_two = second_right(wide_fields)
    table_one = inverse_table(ALPHA_ONE, interior)
    table_two = inverse_table(ALPHA_TWO, interior)
    inner_one = jnp.einsum(
        "ij,sjl->sil",
        jnp.asarray(table_one, jnp.float32),
        right_one[:, :interior],
        precision=lax.Precision.HIGHEST,
        preferred_element_type=jnp.float32,
    )
    inner_two = jnp.einsum(
        "ij,sjl->sil",
        jnp.asarray(table_two, jnp.float32),
        right_two[:, :interior],
        precision=lax.Precision.HIGHEST,
        preferred_element_type=jnp.float32,
    )
    partial_rows = jnp.concatenate([inner_one, inner_two], 0)
    right_sides = jnp.concatenate([right_one, right_two], 0)
    alpha_rows = np.array([ALPHA_ONE] * 4 + [ALPHA_TWO] * 3)
    tables = [table_one] * 4 + [table_two] * 3
    left_cols = np.stack([-alpha_rows[k] * tables[k][:, 0] for k in range(7)])
    right_cols = np.stack([-alpha_rows[k] * tables[k][:, interior - 1] for k in range(7)])
    middle_denominator = (
        1.0 + alpha_rows * right_cols[:, interior - 1] + alpha_rows * left_cols[:, 0]
    )
    end_denominator = 1.0 + alpha_rows * right_cols[:, interior - 1]
    alpha_column = jnp.asarray(alpha_rows, jnp.float32)[:, None]
    middle_column = jnp.asarray(middle_denominator, jnp.float32)[:, None]
    end_column = jnp.asarray(end_denominator, jnp.float32)[:, None]
    first_rows = partial_rows[:, 0]
    last_rows = partial_rows[:, interior - 1]
    edge_rows = right_sides[:, cell_count - 1]
    next_first = shifted(first_rows, "gx", -1)
    denominator = jnp.where(position == group_size - 1, end_column, middle_column)
    own_separator = (edge_rows - alpha_column * last_rows - alpha_column * next_first) / denominator
    left_separator = shifted(own_separator, "gx", 1)
    left_table = jnp.asarray(left_cols, jnp.float32)[:, :, None]
    right_table = jnp.asarray(right_cols, jnp.float32)[:, :, None]
    inner_rows = (
        partial_rows
        + left_separator[:, None, :] * left_table
        + own_separator[:, None, :] * right_table
    )
    solutions = jnp.concatenate([inner_rows, own_separator[:, None, :]], 1)
    velocity_x = stretch * solutions[0]
    field_slope = solutions[1:4]
    field_bend = solutions[4:7]
    field_x = stretch * field_slope
    field_xx = stretch * stretch * field_bend + curving * field_slope
    diffusion = jnp.asarray(np.array([VISCOSITY, VISCOSITY, DIFFUSIVITY]), jnp.float32)[
        :, None, None
    ]
    tendency = -(velocity * field_x + fields * velocity_x) + diffusion * field_xx
    new_register = KEEP_FACTOR * register + time_step * tendency
    new_fields = fields + STEP_FACTOR * new_register
    return (new_fields, new_register, velocity)


def solution(mesh):
    placed = (P(None, "gx", "gz"), P(None, "gx", "gz"), P("gx", "gz"), P("gx"), P("gx"))
    return jax.shard_map(
        local,
        mesh=mesh,
        in_specs=placed,
        out_specs=(P(None, "gx", "gz"), P(None, "gx", "gz"), P("gx", "gz")),
        check_vma=False,
    )
```

profile of v0, /device:TPU:1, one launch (start us, length us, event | category | flops | bytes accessed | tf_op | source)
XLA Modules:
  0.0 210.8 jit_solution(2927979762226832781)
XLA Ops:
  0.6 0.0 copy-start.13
  0.6 0.8 mul.165
  1.4 2.1 %fusion.23 = f32[64,3072]{1,0:T(8,128)S(1)} fusion(f32[64,64]{1,0:T(8,128)} %constant.48.clone, f32[64,3072]{1,0:T(8,128)} %param.16, f32[64]{0:T(128)} %param.17), kind=kOutput, calls=%fused_computation.48 | convolution fusion | flops 151191552 | bytes 1589504 | tf_op jit(solution)/shard_map/dot_general | solution.py:87
  3.5 0.0 copy-start.8
  3.5 0.9 copy-done.8
  4.4 54.9 %all-gather = f32[64,1,3072]{2,1,0:T(1,128)S(1)} all-gather(f32[1,1,3072]{2,1,0:T(1,128)S(1)} %slice_bitcast_fusion), channel_id=1, replica_groups=mesh['gx'=64,'gz'=4] {'gx'}, dimensions={0}, use_global_device_ids=true | all-gather | bytes 798720 | tf_op jit(solution)/shard_map/all_gather | solution.py:94
  59.4 0.3 fusion.22
  59.6 2.2 %add_reduce_fusion = (f32[]{:T(128)}, f32[64,3072]{1,0:T(8,128)S(1)}) fusion(f32[64]{0:T(128)S(1)} %mul.165, f32[64]{0:T(128)S(1)} %copy-done.13, f32[64,3072]{1,0:T(8,128)} %param.16, f32[64,3072]{1,0:T(8,128)} %copy-done.8, f32[3072]{0:T(1024)S(1)} %fusion.22), kind=kLoop, calls=%fused_computation.45 | loop fusion | flops 1769471 | bytes 2372100 | tf_op jit(solution)/shard_map/reduce_max | solution.py:98
  61.9 0.7 fusion.33
  62.6 2.1 collective-permute-start.1
  64.6 3.5 %collective-permute-start = (f32[2,3072]{1,0:T(2,128)}, f32[2,3072]{1,0:T(2,128)}, u32[]{:S(2)}, u32[]{:S(2)}) collective-permute-start(f32[2,3072]{1,0:T(2,128)} %get-tuple-element.17), channel_id=1, source_target_pairs={{0,4},{4,8},{8,12},{12,16},{16,20},{20,24},{24,28},{28,32},{32,36}... | collective-permute-start | bytes 73736 | tf_op jit(solution)/shard_map/ppermute | solution.py:27
  68.1 0.0 copy-done.1
  68.1 1.6 copy.31
  69.8 1.6 copy-done.3
  71.5 1.9 collective-permute-start.2
  73.4 2.6 %collective-permute-start.3 = (f32[3,2,3072]{2,0,1:T(4,128)S(1)}, f32[3,2,3072]{2,0,1:T(4,128)S(1)}, u32[]{:S(2)}, u32[]{:S(2)}) collective-permute-start(f32[3,2,3072]{2,0,1:T(4,128)S(1)} %get-tuple-element.13), channel_id=1, source_target_pairs={{4,0},{8,4},{12,8},{16,12},{20,16},{24,20},{28,24},{32,28},{36,32}... | collective-permute-start | bytes 221192 | tf_op jit(solution)/shard_map/ppermute | solution.py:30
  76.0 0.0 collective-permute-done.1
  76.0 0.0 collective-permute-done
  76.0 0.8 pad_maximum_fusion.2
  76.9 0.6 broadcast_in_dim.18
  77.5 0.0 collective-permute-done.2
  77.5 2.2 %copy_dynamic-update-slice_fusion.1 = (f32[3,66,3072]{2,0,1:T(4,128)S(1)}, f32[3,66,3072]{2,0,1:T(4,128)S(1)}) fusion(f32[3,64,3072]{2,1,0:T(8,128)S(1)} %copy-done.1, f32[3,66,3072]{2,0,1:T(4,128)S(1)} %constant_dynamic-update-slice_fusion.1), kind=kLoop, calls=%fused_computation.59 | loop fusion | bytes 8650752
  79.7 0.0 collective-permute-done.3
  79.8 1.6 maximum_maximum_fusion
  81.3 2.8 %fusion.6 = f32[4,64,3072]{2,0,1:T(4,128)S(1)} fusion(f32[4,68,3072]{2,0,1:T(4,128)S(1)} %maximum_maximum_fusion), kind=kLoop, calls=%fused_computation.21 | loop fusion | flops 3932160 | bytes 15728640 | tf_op jit(solution)/shard_map/add | solution.py:65
  84.2 5.6 %fusion.3 = f32[3,64,3072]{2,0,1:T(4,128)S(1)} fusion(f32[3,66,3072]{2,0,1:T(4,128)S(1)} %get-tuple-element.16, f32[3,66,3072]{2,0,1:T(4,128)S(1)} %constant_dynamic-update-slice_fusion, f32[3,64,3072]{2,1,0:T(8,128)S(1)} %copy-done.1), kind=kLoop, calls=%fused_computation.14 | loop fusion | flops 4718592 | bytes 14155776 | tf_op jit(solution)/shard_map/add | solution.py:74
  89.8 0.0 copy-start.12
  89.8 0.5 slice.102
  90.4 0.2 copy-done.12
  90.6 3.7 %fusion.17 = f32[3,3072,63]{1,2,0:T(8,128)S(1)} fusion(f32[63,63,1]{1,0,2:T(8,128)S(1)} %copy-done.12, f32[3,63,3072]{2,0,1:T(4,128)S(1)} %slice.102), kind=kOutput, calls=%fused_computation.36 | convolution fusion | flops 438939648 | bytes 4660740 | tf_op jit(solution)/shard_map/ij,sjl->sil/dot_general | solution.py:114
  94.3 1.6 copy.53
  95.9 0.0 copy-start.11
  95.9 0.2 slice.97
  96.2 0.6 copy-done.11
  96.7 5.3 %fusion.8 = f32[4,3072,63]{1,2,0:T(8,128)S(1)} fusion(f32[63,63,1]{1,0,2:T(8,128)S(1)} %copy-done.11, f32[4,63,3072]{2,0,1:T(4,128)S(1)} %slice.97), kind=kOutput, calls=%fused_computation.24 | convolution fusion | flops 585252864 | bytes 6209028 | tf_op jit(solution)/shard_map/ij,sjl->sil/dot_general | solution.py:107
  102.0 2.3 %copy.54 = f32[4,3072,63]{1,0,2:T(4,128)S(1)} copy(f32[4,3072,63]{1,2,0:T(8,128)S(1)} %fusion.8) | data formatting | bytes 6193152 | tf_op jit(solution)/shard_map/ij,sjl->sil/dot_general | solution.py:107
  104.3 0.0 copy-start.17
  104.3 0.0 copy-start.18
  104.3 0.0 copy-start.16
  104.3 1.9 collective-permute-start.4
  106.3 0.0 copy-start.9
  106.3 0.0 copy-start.10
  106.3 3.9 %collective-permute-done.4 = f32[7,3072]{1,0:T(8,128)S(1)} collective-permute-done((f32[7,3072]{1,0:T(8,128)S(1)}, f32[7,3072]{1,0:T(8,128)S(1)}, u32[]{:S(2)}, u32[]{:S(2)}) %collective-permute-start.4) | collective-permute-done | bytes 86048 | tf_op jit(solution)/shard_map/ppermute | solution.py:38
  110.3 0.0 copy-done
  110.3 0.1 fusion.29
  110.4 1.9 collective-permute-start.5
  112.3 84.8 %pmax.7 = f32[]{:T(128)} all-reduce(f32[]{:T(128)} %get-tuple-element.11), channel_id=1, replica_groups=mesh['gx'=64,'gz'=4] {'gx','gz'}, use_global_device_ids=true, to_apply=%region_2.3 | all-reduce | flops 1 | bytes 8 | tf_op jit(solution)/shard_map/pmax | solution.py:99
  197.8 0.1 broadcast_in_dim.19
  197.9 0.0 collective-permute-done.5
  197.9 0.0 copy-done.9
  197.9 0.0 copy-done.10
  197.9 3.4 %fusion.1 = f32[7,63,3072]{2,0,1:T(8,128)S(1)} fusion(f32[3,63,3072]{2,0,1:T(4,128)} %bitcast.38, f32[4,63,3072]{2,0,1:T(4,128)S(1)} %bitcast.35, f32[7,63]{0,1:T(8,128)S(1)} %copy-done.9, f32[7,3072]{1,0:T(8,128)S(1)} %fusion.29, f32[7,63]{0,1:T(8,128)S(1)} %copy-done.10, f32[7,3072]{1,0:T(8,128)S(1)} %collective-permute-done.5), kind=kLoop, calls=%fused_computation.8 | loop fusion | flops 6773760 | bytes 11013576 | tf_op jit(solution)/shard_map/add | solution.py:144
  201.3 3.1 %copy.41 = f32[7,63,3072]{2,1,0:T(8,128)S(1)} copy(f32[7,63,3072]{2,0,1:T(8,128)S(1)} %fusion.1) | data formatting | bytes 10838016 | tf_op jit(solution)/shard_map/add | solution.py:144
  204.5 0.0 copy-start.2
  204.5 0.0 copy-start.6
  204.5 0.0 copy-start.7
  204.5 0.0 copy-start.14
  204.5 0.0 copy-start.15
  204.5 0.1 fusion.21
  204.7 1.5 copy-done.2
  206.1 0.2 copy-done.6
  206.3 0.8 copy-done.7
  207.1 0.0 copy-done.15
  207.1 3.7 %multiply_add_fusion = (f32[3,64,3072]{2,1,0:T(8,128)}, f32[3,64,3072]{2,1,0:T(8,128)}) fusion(f32[3,64,3072]{2,1,0:T(8,128)S(1)} %copy-done.2, f32[64]{0:T(128)S(1)} %copy-done.14, f32[7,1,3072]{2,1,0:T(1,128)S(1)} %broadcast_in_dim.19, f32[7,63,3072]{2,1,0:T(8,128)S(1)} %copy.41, f32[64]{0:T(128)S(1)} %mul.165, f32[3]{0:T(128)S(1)} %copy-done.15, ...), kind=kLoop, calls=%fused_computation.38 | loop fusion | flops 10027008 | bytes 16515856 | tf_op jit(solution)/shard_map/add | solution.py:159
  (19 shorter events, 0.2 us)
Async XLA Ops:
  0.6 59.0 %copy-start.13 = (f32[64]{0:T(128)S(1)}, f32[64]{0:T(128)}, u32[]{:S(2)}) copy-start(f32[64]{0:T(128)} %param.17) | copy-start | bytes 772
  1.4 66.7 %copy-start.1 = (f32[3,64,3072]{2,1,0:T(8,128)S(1)}, f32[3,64,3072]{2,1,0:T(8,128)}, u32[]{:S(2)}) copy-start(f32[3,64,3072]{2,1,0:T(8,128)} %param.14) | copy-start | bytes 7077892
  3.5 0.9 copy-start.8
  61.9 15.0 %copy-start.5 = (f32[64,3072]{1,0:T(8,128)}, f32[64,3072]{1,0:T(8,128)S(1)}, u32[]{:S(2)}) copy-start(f32[64,3072]{1,0:T(8,128)S(1)} %get-tuple-element.12) | copy-start | bytes 2359300
  62.6 13.4 %collective-permute-start.1 = (f32[2,3072]{1,0:T(2,128)}, f32[2,3072]{1,0:T(2,128)}, u32[]{:S(2)}, u32[]{:S(2)}) collective-permute-start(f32[2,3072]{1,0:T(2,128)} %get-tuple-element.18), channel_id=1, source_target_pairs={{4,0},{8,4},{12,8},{16,12},{20,16},{24,20},{28,24},{32,28},{36,32}... | collective-permute-start | bytes 73736 | tf_op jit(solution)/shard_map/ppermute | solution.py:30
  64.6 11.4 %collective-permute-start = (f32[2,3072]{1,0:T(2,128)}, f32[2,3072]{1,0:T(2,128)}, u32[]{:S(2)}, u32[]{:S(2)}) collective-permute-start(f32[2,3072]{1,0:T(2,128)} %get-tuple-element.17), channel_id=1, source_target_pairs={{0,4},{4,8},{8,12},{12,16},{16,20},{20,24},{24,28},{28,32},{32,36}... | collective-permute-start | bytes 73736 | tf_op jit(solution)/shard_map/ppermute | solution.py:27
  69.8 1.7 copy-start.3
  71.5 6.0 %collective-permute-start.2 = (f32[3,2,3072]{2,0,1:T(4,128)S(1)}, f32[3,2,3072]{2,0,1:T(4,128)S(1)}, u32[]{:S(2)}, u32[]{:S(2)}) collective-permute-start(f32[3,2,3072]{2,0,1:T(4,128)S(1)} %get-tuple-element.14), channel_id=1, source_target_pairs={{0,4},{4,8},{8,12},{12,16},{16,20},{20,24},{24,28},{28,32},{32,36}... | collective-permute-start | bytes 221192 | tf_op jit(solution)/shard_map/ppermute | solution.py:27
  73.4 6.3 %collective-permute-start.3 = (f32[3,2,3072]{2,0,1:T(4,128)S(1)}, f32[3,2,3072]{2,0,1:T(4,128)S(1)}, u32[]{:S(2)}, u32[]{:S(2)}) collective-permute-start(f32[3,2,3072]{2,0,1:T(4,128)S(1)} %get-tuple-element.13), channel_id=1, source_target_pairs={{4,0},{8,4},{12,8},{16,12},{20,16},{24,20},{28,24},{32,28},{36,32}... | collective-permute-start | bytes 221192 | tf_op jit(solution)/shard_map/ppermute | solution.py:30
  77.5 2.3 %copy-start.4 = (f32[3,64,3072]{2,0,1:T(4,128)S(1)}, f32[3,64,3072]{2,0,1:T(4,128)}, u32[]{:S(2)}) copy-start(f32[3,64,3072]{2,0,1:T(4,128)} %copy-done.3) | copy-start | bytes 7077892
  89.8 0.8 copy-start.12
  95.9 14.3 %copy-start = (f32[3,3072,63]{1,0,2:T(4,128)}, f32[3,3072,63]{1,0,2:T(4,128)S(1)}, u32[]{:S(2)}) copy-start(f32[3,3072,63]{1,0,2:T(4,128)S(1)} %copy.53) | copy-start | bytes 6967300
  95.9 0.8 copy-start.11
  104.3 2.0 copy-start.17
  104.3 2.0 copy-start.18
  104.3 6.0 %copy-start.16 = (f32[7]{0:T(128)S(1)}, f32[7]{0:T(128)}, u32[]{:S(2)}) copy-start(f32[7]{0:T(128)} %constant.51.clone) | copy-start | bytes 88
  104.3 5.9 %collective-permute-start.4 = (f32[7,3072]{1,0:T(8,128)S(1)}, f32[7,3072]{1,0:T(8,128)S(1)}, u32[]{:S(2)}, u32[]{:S(2)}) collective-permute-start(f32[7,3072]{1,0:T(8,128)S(1)} %fusion.30), channel_id=1, source_target_pairs={{4,0},{8,4},{12,8},{16,12},{20,16},{24,20},{28,24},{32,28},{36,32}... | collective-permute-start | bytes 258056 | tf_op jit(solution)/shard_map/ppermute | solution.py:38
  106.3 91.6 %copy-start.9 = (f32[7,63]{0,1:T(8,128)S(1)}, f32[7,63]{0,1:T(8,128)}, u32[]{:S(2)}) copy-start(f32[7,63]{0,1:T(8,128)} %constant.55.clone) | copy-start | bytes 5296
  106.3 91.6 %copy-start.10 = (f32[7,63]{0,1:T(8,128)S(1)}, f32[7,63]{0,1:T(8,128)}, u32[]{:S(2)}) copy-start(f32[7,63]{0,1:T(8,128)} %constant.54.clone) | copy-start | bytes 5296
  110.4 87.5 %collective-permute-start.5 = (f32[7,3072]{1,0:T(8,128)S(1)}, f32[7,3072]{1,0:T(8,128)S(1)}, u32[]{:S(2)}, u32[]{:S(2)}) collective-permute-start(f32[7,3072]{1,0:T(8,128)S(1)} %fusion.29), channel_id=1, source_target_pairs={{0,4},{4,8},{8,12},{12,16},{16,20},{20,24},{24,28},{28,32},{32,36}... | collective-permute-start | bytes 258056 | tf_op jit(solution)/shard_map/ppermute | solution.py:38
  204.5 1.7 copy-start.2
  204.5 1.8 copy-start.6
  204.5 2.6 %copy-start.7 = (f32[3,64,3072]{2,1,0:T(8,128)S(1)}, f32[3,64,3072]{2,1,0:T(8,128)}, u32[]{:S(2)}) copy-start(f32[3,64,3072]{2,1,0:T(8,128)} %param.15) | copy-start | bytes 7077892
  204.5 2.6 %copy-start.14 = (f32[64]{0:T(128)S(1)}, f32[64]{0:T(128)}, u32[]{:S(2)}) copy-start(f32[64]{0:T(128)} %param.18) | copy-start | bytes 772
  204.5 2.6 %copy-start.15 = (f32[3]{0:T(128)S(1)}, f32[3]{0:T(128)}, u32[]{:S(2)}) copy-start(f32[3]{0:T(128)} %constant.56.clone) | copy-start | bytes 40
where the time goes:
time: 211 us
  blocking collectives  140 us (66%)
  other arithmetic  21.4 us (10%)
  local copies, waits for them, and re-layouts  18.8 us (9%)
  starting transfers between devices  13.9 us (7%)
  matrix products  11.1 us (5%)
  waiting for transfers between devices  3.96 us (2%)
    pmax x1, blocking collectives, local(): max_rate = lax.pmax(local_rate, ('gx', 'gz'))  84.8 us
    all_gather x1, blocking collectives, local(): gathered = lax.all_gather(totals, 'gx', axis=0, tiled=True)  54.9 us
    unnamed x42, local copies, waits for them, and re-layouts  9.68 us
    add x1, other arithmetic, second_right(): return COEF_TWO * near + WIDE_TWO / 4.0 * far  5.61 us
    ppermute x2, starting transfers between devices, with_halo(): lax.ppermute(lax.slice_in_dim(block, block.shape[dim] - width, None, axis...  5.41 us
    dot_general x1, matrix products, local(): jnp.einsum('ij,sjl->sil', jnp.asarray(table_one, jnp.float32), right_one[...  5.26 us
    ppermute x2, starting transfers between devices, with_halo(): lax.ppermute(lax.slice_in_dim(block, 0, width, axis=dim), axis, backward)  4.65 us
  transfers between devices with their start and end apart: 6, of which 1 were waited for; matrix products, arithmetic and copies ran while one was open for 3% of the time, Pallas kernels for 0%

commit v1 on v0

v1 whole, which is shorter than its diff:
```python
import functools

import jax
import jax.numpy as jnp
import numpy as np
from jax import lax
from jax.experimental import pallas as pl
from jax.experimental.pallas import tpu as pltpu
from jax.sharding import Mesh
from jax.sharding import PartitionSpec as P

ALPHA_ONE = 1.0 / 3.0
COEF_ONE = 14.0 / 9.0
WIDE_ONE = 1.0 / 9.0
ALPHA_TWO = 2.0 / 11.0
COEF_TWO = 12.0 / 11.0
WIDE_TWO = 3.0 / 11.0
VISCOSITY = 0.25
DIFFUSIVITY = 0.2
COURANT = 1.2
KEEP_FACTOR = -5.0 / 9.0
STEP_FACTOR = 15.0 / 16.0

LANES = 128
CHUNK = 1024
MESSAGE = 16
DEPTH = 256


def inverse(alpha, length):
    matrix = np.eye(length) + alpha * (np.eye(length, k=1) + np.eye(length, k=-1))
    return np.linalg.inv(matrix)


@functools.cache
def operators(cells):
    length = 4 * cells
    near_up, near_down = np.eye(length, k=1), np.eye(length, k=-1)
    far_up, far_down = np.eye(length, k=2), np.eye(length, k=-2)
    first = COEF_ONE / 2.0 * (near_up - near_down) + WIDE_ONE / 4.0 * (far_up - far_down)
    second = COEF_TWO * (near_up - 2.0 * np.eye(length) + near_down) + WIDE_TWO / 4.0 * (
        far_up - 2.0 * np.eye(length) + far_down
    )
    slope = inverse(ALPHA_ONE, length) @ first
    bend = inverse(ALPHA_TWO, length) @ second
    integral = -(np.tril(np.ones((length, length))) - 0.5 * np.eye(length))
    constant = slope @ np.ones(length)
    return slope, bend, slope @ integral, constant


def from_left(matrix, block, cells):
    start = block * cells
    part = matrix[start : start + cells, start - cells : start]
    weights = part[1]
    factors = part[:, cells - 2] / part[1, cells - 2]
    corner = np.zeros(cells)
    corner[0] = part[0, cells - 1] - factors[0] * part[1, cells - 1]
    return factors, weights, corner


def from_right(matrix, block, cells):
    start = block * cells
    part = matrix[start : start + cells, start + cells : start + 2 * cells]
    weights = part[cells - 2]
    factors = part[:, 1] / part[cells - 2, 1]
    corner = np.zeros(cells)
    corner[cells - 1] = part[cells - 1, 0] - factors[cells - 1] * part[cells - 2, 0]
    return factors, weights, corner


@functools.cache
def tables(cells):
    slope, bend, drift, constant = operators(cells)
    kinds = (0, 2, 1, 3)
    send = np.zeros((4, cells, LANES))
    solve = np.zeros((4, 3, cells, DEPTH))
    for kind, block in enumerate(kinds):
        odd = kind >= 2
        start = block * cells
        own = slice(start, start + cells)
        rest = np.zeros(4 * cells)
        if block == 3:
            rest[own] = constant[own]
        local = drift + rest[:, None] * (np.arange(4 * cells) < start)[None, :]
        for which, matrix in enumerate((slope, bend, local)):
            base = np.zeros((cells, cells + 8))
            base[:, :cells] = matrix[own, own]
            left, right = (0, 4) if odd else (4, 0)
            slot = 1 if which == 1 else 0
            if block > 0:
                factors, _, corner = from_left(matrix, block, cells)
                base[:, cells + left + slot] = factors
                base[:, cells + left + 2] = corner
            if block < 3:
                factors, _, corner = from_right(matrix, block, cells)
                base[:, cells + right + slot] = factors
                base[:, cells + right + 2] = corner
            if which == 2:
                base[:, cells + 1] = -rest[own]
            for copy in range(3):
                solve[kind, which, :, copy * cells : (copy + 1) * cells] = base[:, :cells]
                solve[kind, which, :, 3 * cells + 8 * copy : 3 * cells + 8 * copy + 8] = base[:, cells:]
            to_right = to_left = np.zeros(cells)
            sent = (slope, bend, drift)[which]
            if block < 2:
                to_right = from_left(sent, block + 1, cells)[1]
            elif block == 2:
                to_right = from_left(sent, 2, cells)[1]
            if block > 0:
                to_left = from_right(sent, block - 1, cells)[1]
            pair = (to_left, to_right) if odd else (to_right, to_left)
            send[kind, :, which] = pair[0]
            send[kind, :, 3 + which] = pair[1]
    return send.astype(np.float32), solve.astype(np.float32)


def column(row):
    size = row.shape[1]
    rows = lax.broadcasted_iota(jnp.int32, (size, size), 0)
    columns = lax.broadcasted_iota(jnp.int32, (size, size), 1)
    spread = jnp.broadcast_to(row, (size, size))
    return jnp.sum(jnp.where(rows == columns, spread, 0.0), axis=1, keepdims=True)


def halves(value):
    high = value.astype(jnp.bfloat16)
    low = (value - high.astype(jnp.float32)).astype(jnp.bfloat16)
    return high, low


def send_kernel(where, fields, source, metric, weights, totals, message_one, message_two):
    cells = source.shape[0]
    odd = where[0] >= 2
    scaled = source[...] * (1.0 / column(metric[...]))
    total = jnp.sum(scaled, axis=0, keepdims=True)
    for peer in range(totals.shape[0]):
        for k in range(CHUNK // LANES):
            totals[peer, k : k + 1, :] = total[:, k * LANES : (k + 1) * LANES]
    blank = jnp.zeros((1, CHUNK), jnp.float32)
    for k in range(4):
        value = fields[k] if k < 3 else scaled
        first, last = value[:1], value[cells - 1 :]
        for message, begin in ((message_one, 0), (message_two, 3)):
            row = 4 * k
            if k < 3:
                for which in range(2):
                    weight = weights[0, :, begin + which : begin + which + 1]
                    message[row + which : row + which + 1, :] = jnp.sum(value * weight, axis=0, keepdims=True)
            else:
                weight = weights[0, :, begin + 2 : begin + 3]
                message[row : row + 1, :] = jnp.sum(value * weight, axis=0, keepdims=True)
                message[row + 1 : row + 2, :] = blank
            edge = jnp.where(odd, first, last) if begin == 0 else jnp.where(odd, last, first)
            message[row + 2 : row + 3, :] = edge
            message[row + 3 : row + 4, :] = blank


def velocity_kernel(place, source, metric, inner, outer, lower, velocity, offset, rate, peak):
    step = pl.program_id(0)
    stretch = column(metric[...])
    scaled = source[...] * (1.0 / stretch)
    high = scaled.astype(jnp.bfloat16)
    rest = scaled - high.astype(jnp.float32)
    middle = rest.astype(jnp.bfloat16)
    low = (rest - middle.astype(jnp.float32)).astype(jnp.bfloat16)
    pieces = jnp.concatenate([high, middle, low], axis=0)
    running = jnp.dot(lower[...], pieces, preferred_element_type=jnp.float32)
    before = jnp.zeros((CHUNK // LANES, LANES), jnp.float32)
    for peer in range(inner.shape[0]):
        before += jnp.where(peer < place[0], inner[peer], 0.0)
    for peer in range(outer.shape[0]):
        before += jnp.where(peer < place[1], outer[peer], 0.0)
    shift = jnp.concatenate([before[k : k + 1, :] for k in range(CHUNK // LANES)], axis=1)
    offset[...] = shift
    value = -(running + shift)
    velocity[...] = value
    here = jnp.abs(value) * stretch + 4.0 * VISCOSITY * stretch * stretch
    top = jnp.max(jnp.max(here, axis=0, keepdims=True), axis=1, keepdims=True)

    @pl.when(step == 0)
    def _():
        peak[...] = jnp.broadcast_to(top, peak.shape)

    @pl.when(step > 0)
    def _():
        peak[...] = jnp.maximum(peak[...], top)

    @pl.when(step == pl.num_programs(0) - 1)
    def _():
        rate[...] = jnp.broadcast_to(peak[:1, :], rate.shape)


def update_kernel(
    where, fields, register, source, velocity, offset, message_one, message_two, metric, curvature, rates, table,
    new_fields, new_register, mixed, mixed_scalar, drift,
):
    cells = source.shape[0]
    stretch = column(metric[...])

    @pl.when(pl.program_id(0) == 0)
    def _():
        curving = column(curvature[...])
        slope, bend = table[0, 0], table[0, 1]
        lane = lax.broadcasted_iota(jnp.int32, (cells, DEPTH), 1)
        is_low = ((lane >= 2 * cells) & (lane < 3 * cells)) | (lane >= 3 * cells + 16)

        def split(value):
            high, low = halves(value)
            return jnp.where(is_low, low.astype(jnp.float32), high.astype(jnp.float32)).astype(jnp.bfloat16)

        field_x = stretch * slope
        field_xx = stretch * stretch * bend + curving * slope
        mixed[:cells, :] = split(field_x)
        mixed[cells:, :] = split(VISCOSITY * field_xx)
        mixed_scalar[:cells, :] = mixed[:cells, :]
        mixed_scalar[cells:, :] = split(DIFFUSIVITY * field_xx)
        drift[...] = split(stretch * table[0, 2])

    def stacked(value, tail):
        high, low = halves(value)
        tail_high = tail.astype(jnp.bfloat16).astype(jnp.float32)
        tail_low = tail - tail_high
        tails = jnp.concatenate(
            [tail_high, tail_low, tail_high, jnp.zeros((DEPTH - 3 * cells - 24, CHUNK), jnp.float32)], axis=0
        ).astype(jnp.bfloat16)
        return jnp.concatenate([high, low, high, tails], axis=0)

    time_step = COURANT / jnp.max(jnp.max(rates[...], axis=0, keepdims=True), axis=1, keepdims=True)
    scaled = source[...] * (1.0 / stretch)
    lead = message_one[12:16, :]
    row = lax.broadcasted_iota(jnp.int32, lead.shape, 0)
    lead = jnp.where(row == 1, offset[...], lead)
    tail = jnp.concatenate([lead, message_two[12:16, :]], axis=0)
    velocity_x = jnp.dot(drift[...], stacked(scaled, tail), preferred_element_type=jnp.float32)
    speed = velocity[...]
    for k in range(3):
        field = fields[k]
        tail = jnp.concatenate([message_one[4 * k : 4 * k + 4, :], message_two[4 * k : 4 * k + 4, :]], axis=0)
        weights = mixed if k < 2 else mixed_scalar
        both = jnp.dot(weights[...], stacked(field, tail), preferred_element_type=jnp.float32)
        tendency = both[cells:] - (speed * both[:cells] + field * velocity_x)
        updated = KEEP_FACTOR * register[k] + time_step * tendency
        new_register[k] = updated
        new_fields[k] = field + STEP_FACTOR * updated


def local(fields, register, source, metric, curvature):
    cells, lines = source.shape
    steps = lines // CHUNK
    count = lax.axis_size(("slab", "inner"))
    inner_count, slab_count = lax.axis_size("inner"), lax.axis_size("slab")
    devices = count * lax.axis_size("gz")
    inner, slab = lax.axis_index("inner"), lax.axis_index("slab")
    position = slab * inner_count + inner
    kind = jnp.where(position == 0, 0, jnp.where(position == count - 1, 3, 1 + position % 2))
    where = jnp.reshape(kind, (1,)).astype(jnp.int32)
    place = jnp.stack([inner, slab]).astype(jnp.int32)
    send_weights, solve_tables = tables(cells)
    metric_row, curvature_row = metric[None, :], curvature[None, :]

    by_field = pl.BlockSpec((3, cells, CHUNK), lambda i, s: (0, 0, i))
    by_line = pl.BlockSpec((cells, CHUNK), lambda i, s: (0, i))
    by_row = pl.BlockSpec((1, cells), lambda i, s: (0, 0))
    by_message = pl.BlockSpec((MESSAGE, CHUNK), lambda i, s: (0, i))
    by_total = pl.BlockSpec((inner_count, CHUNK // LANES, LANES), lambda i, s: (0, i, 0))
    by_slab = pl.BlockSpec((slab_count, CHUNK // LANES, LANES), lambda i, s: (0, i, 0))
    by_offset = pl.BlockSpec((1, CHUNK), lambda i, s: (0, i))

    def shape(*sizes):
        return jax.ShapeDtypeStruct(sizes, jnp.float32)

    totals, message_one, message_two = pl.pallas_call(
        send_kernel,
        grid_spec=pltpu.PrefetchScalarGridSpec(
            num_scalar_prefetch=1,
            grid=(steps,),
            in_specs=[by_field, by_line, by_row, pl.BlockSpec((1, cells, LANES), lambda i, s: (s[0], 0, 0))],
            out_specs=[by_total, by_message, by_message],
        ),
        out_shape=[shape(inner_count, lines // LANES, LANES), shape(MESSAGE, lines), shape(MESSAGE, lines)],
        name="send",
    )(where, fields, source, metric_row, jnp.asarray(send_weights))

    line = ("slab", "inner")
    even_pairs = [(i, i ^ 1) for i in range(count)]
    odd_pairs = [(i, i + 1 if i % 2 else i - 1) for i in range(1, count - 1)]
    got_one = lax.ppermute(message_one, line, even_pairs)
    got_two = lax.ppermute(message_two, line, odd_pairs)

    inner_totals = lax.all_to_all(totals, "inner", 0, 0)
    slab_total = jnp.sum(inner_totals, axis=0, keepdims=True)
    slab_totals = lax.all_to_all(jnp.broadcast_to(slab_total, (slab_count, *slab_total.shape[1:])), "slab", 0, 0)

    lower = np.tril(np.ones((cells, cells))) - 0.5 * np.eye(cells)
    lower = jnp.asarray(np.concatenate([lower] * 3, axis=1), jnp.bfloat16)
    velocity, offset, rate = pl.pallas_call(
        velocity_kernel,
        grid_spec=pltpu.PrefetchScalarGridSpec(
            num_scalar_prefetch=1,
            grid=(steps,),
            in_specs=[by_line, by_row, by_total, by_slab, pl.BlockSpec((cells, 3 * cells), lambda i, s: (0, 0))],
            out_specs=[by_line, by_offset, pl.BlockSpec((devices, LANES), lambda i, s: (0, 0))],
            scratch_shapes=[pltpu.VMEM((8, LANES), jnp.float32)],
        ),
        out_shape=[shape(cells, lines), shape(1, lines), shape(devices, LANES)],
        name="velocity",
    )(place, source, metric_row, inner_totals, slab_totals, lower)

    rates = lax.all_to_all(rate, ("slab", "inner", "gz"), 0, 0, tiled=True)

    new_fields, new_register = pl.pallas_call(
        update_kernel,
        grid_spec=pltpu.PrefetchScalarGridSpec(
            num_scalar_prefetch=1,
            grid=(steps,),
            in_specs=[
                by_field, by_field, by_line, by_line, by_offset, by_message, by_message, by_row, by_row,
                pl.BlockSpec((devices, LANES), lambda i, s: (0, 0)),
                pl.BlockSpec((1, 3, cells, DEPTH), lambda i, s: (s[0], 0, 0, 0)),
            ],
            out_specs=[by_field, by_field],
            scratch_shapes=[
                pltpu.VMEM((2 * cells, DEPTH), jnp.bfloat16),
                pltpu.VMEM((2 * cells, DEPTH), jnp.bfloat16),
                pltpu.VMEM((cells, DEPTH), jnp.bfloat16),
            ],
        ),
        out_shape=[shape(3, cells, lines), shape(3, cells, lines)],
        compiler_params=pltpu.CompilerParams(vmem_limit_bytes=32 * 1024 * 1024),
        name="update",
    )(
        where, fields, register, source, velocity, offset, got_one, got_two, metric_row, curvature_row, rates,
        jnp.asarray(solve_tables),
    )
    return (new_fields, new_register, velocity)


def solution(mesh):
    along, across = mesh.devices.shape
    inner = 1
    while inner * inner < along:
        inner *= 2
    split = Mesh(mesh.devices.reshape(along // inner, inner, across), ("slab", "inner", "gz"))
    line = ("slab", "inner")
    placed = (P(None, line, "gz"), P(None, line, "gz"), P(line, "gz"), P(line), P(line))
    return jax.shard_map(
        local,
        mesh=split,
        in_specs=placed,
        out_specs=(P(None, line, "gz"), P(None, line, "gz"), P(line, "gz")),
        check_vma=False,
    )
```

time: 211 us -> 68 us (0.32)
  blocking collectives: 140 us -> 11.5 us
  other arithmetic: 21.4 us -> 0.65 us
  Pallas kernels: 0 us -> 12.7 us
  local copies, waits for them, and re-layouts: 18.8 us -> 7.55 us
  matrix products: 11.1 us -> 0 us
  waiting for transfers between devices: 3.96 us -> 14.9 us
  starting transfers between devices: 13.9 us -> 19.4 us
    pmax x1 -> x0, blocking collectives: 84.8 us -> none  [local(): max_rate = lax.pmax(local_rate, ('gx', 'gz'))]
    all_gather x1 -> x0, blocking collectives: 54.9 us -> none  [local(): gathered = lax.all_gather(totals, 'gx', axis=0, tiled=True)]
    add x4 -> x0, other arithmetic: 15.5 us -> none  [the longest x1 5.61 us: second_right(): return COEF_TWO * near + WIDE_TWO / 4.0 * far]
    all_to_all x0 -> x2, starting transfers between devices: none -> 15.3 us  [the longest x1 7.83 us: local(): rates = lax.all_to_all(rate, ('slab', 'inner', 'gz'), 0, 0, tiled=True)]
    pallas_call x0 -> x3, Pallas kernels: none -> 12.7 us  [the longest x1 4.31 us: local(): pl.pallas_call(send_kernel, grid_spec=pltpu.PrefetchScalarGridSpec(num_sc...]
    all_to_all x0 -> x1, blocking collectives: none -> 11.5 us  [local(): inner_totals = lax.all_to_all(totals, 'inner', 0, 0)]
    dot_general x3 -> x0, matrix products: 11.1 us -> none  [the longest x1 5.26 us: local(): jnp.einsum('ij,sjl->sil', jnp.asarray(table_one, jnp.float32), right_one[...]
    ppermute x6 -> x2, starting transfers between devices: 13.9 us -> 4.14 us  [the longest x1 2.23 us: local(): got_one = lax.ppermute(message_one, line, even_pairs)]
  transfers between devices with their start and end apart: 6 -> 4, of which waited for: 1 -> 3; matrix products, arithmetic and copies ran while one was open for 3% -> 1% of each run, Pallas kernels for 0% -> 0%
where the time goes in v1:
time: 68 us; the launch traced here: 67.5 us
  starting transfers between devices  19.4 us (29%)
  waiting for transfers between devices  14.9 us (22%)
  Pallas kernels  12.7 us (19%)
  blocking collectives  11.5 us (17%)
  local copies, waits for them, and re-layouts  7.55 us (11%)
  between operations  0.75 us (1%)
    all_to_all x1, blocking collectives, local(): inner_totals = lax.all_to_all(totals, 'inner', 0, 0)  11.5 us
    all_to_all x1, starting transfers between devices, local(): rates = lax.all_to_all(rate, ('slab', 'inner', 'gz'), 0, 0, tiled=True)  7.83 us
    all_to_all x1, starting transfers between devices, local(): lax.all_to_all(jnp.broadcast_to(slab_total, (slab_count, *slab_total.shap...  7.48 us
    all_to_all x1, waiting for transfers between devices, local(): lax.all_to_all(jnp.broadcast_to(slab_total, (slab_count, *slab_total.shap...  7.04 us
    unnamed x24, local copies, waits for them, and re-layouts  6.9 us
    ppermute x1, waiting for transfers between devices, local(): got_two = lax.ppermute(message_two, line, odd_pairs)  5.77 us
    pallas_call x1, Pallas kernels, local(): pl.pallas_call(send_kernel, grid_spec=pltpu.PrefetchScalarGridSpec(num_sc...  4.31 us
    pallas_call x1, Pallas kernels, local(): pl.pallas_call(velocity_kernel, grid_spec=pltpu.PrefetchScalarGridSpec(nu...  4.27 us
  transfers between devices with their start and end apart: 4, of which 3 were waited for; matrix products, arithmetic and copies ran while one was open for 1% of the time, Pallas kernels for 0%

profile of v1, /device:TPU:1, one launch (start us, length us, event | category | flops | bytes accessed | tf_op | source)
XLA Modules:
  0.0 67.5 jit_solution(9366836812956919925)
XLA Ops:
  0.7 0.0 copy-start
  0.7 0.0 copy-start.1
  0.7 0.0 copy-start.8
  0.7 0.0 copy-start.9
  0.7 4.3 %send.1 = (f32[8,24,128]{2,1,0:T(8,128)}, f32[16,3072]{1,0:T(8,128)}, f32[16,3072]{1,0:T(8,128)}) custom-call(s32[1]{0:T(128)} %bitcast.where, f32[3,64,3072]{2,1,0:T(8,128)} %fields.3, f32[64,3072]{1,0:T(8,128)} %source.5, f32[1,64]{1,0:T(1,128)} %bitcast.10, f32[4,64,128]{2,1,0:T(8,128)} %constant.39.clone.weights), custom_call_target="tpu_custom_call" | custom-call | tf_op jit(solution)/shard_map/send/pallas_call | solution.py:272
  5.0 11.5 %all_to_all.21.inner = f32[8,24,128]{2,1,0:T(8,128)S(1)} all-to-all(f32[8,24,128]{2,1,0:T(8,128)} %get-tuple-element.11), channel_id=1, replica_groups=mesh['slab'=8,'inner'=8,'gz'=4] {'inner'}, dimensions={0} | all-to-all | bytes 196608 | tf_op jit(solution)/shard_map/all_to_all | solution.py:290
  16.5 0.0 copy-start.10
  16.5 0.7 broadcast_in_dim.13
  17.2 7.5 %all-to-all-start.1 = ((f32[8,24,128]{2,1,0:T(8,128)}), f32[8,24,128]{2,1,0:T(8,128)S(1)}, u32[]{:S(2)}, u32[]{:S(2)}) async-start(f32[8,24,128]{2,1,0:T(8,128)} %broadcast_in_dim.13), calls=%async_computation.1 | async-start | bytes 196608 | tf_op jit(solution)/shard_map/all_to_all | solution.py:292
  24.6 0.6 pad_add_fusion.place
  25.3 7.0 %all-to-all-done.1.outer = f32[8,24,128]{2,1,0:T(8,128)S(1)} async-done(((f32[8,24,128]{2,1,0:T(8,128)}), f32[8,24,128]{2,1,0:T(8,128)S(1)}, u32[]{:S(2)}, u32[]{:S(2)}) %all-to-all-start.1) | async-done | bytes 98336 | tf_op jit(solution)/shard_map/all_to_all | solution.py:292
  32.3 0.0 copy-done.10
  32.3 0.0 copy-start.11
  32.3 0.6 copy-done.11
  33.0 4.3 %velocity.1 = (f32[64,3072]{1,0:T(8,128)}, f32[1,3072]{1,0:T(1,128)}, f32[256,128]{1,0:T(8,128)}) custom-call(s32[2]{0:T(128)} %pad_add_fusion.place, f32[64,3072]{1,0:T(8,128)} %source.5, f32[1,64]{1,0:T(1,128)} %bitcast.11, f32[8,24,128]{2,1,0:T(8,128)} %copy-done.10, f32[8,24,128]{2,1,0:T(8,128)} %copy-done.11, bf16[64,192]{1,0:T(8,128)(2,1)} %constant.40.clone.lower), custom_call_target="tpu_custom_call" | custom-call | tf_op jit(solution)/shard_map/velocity/pallas_call | solution.py:296
  37.2 7.8 %all-to-all-start.2 = ((f32[256,1,128]{2,1,0:T(1,128)}), f32[256,1,128]{2,1,0:T(1,128)S(1)}, u32[]{:S(2)}, u32[]{:S(2)}) async-start(f32[256,1,128]{2,1,0:T(1,128)} %bitcast.14), calls=%async_computation.2 | async-start | bytes 262144 | tf_op jit(solution)/shard_map/all_to_all | solution.py:309
  45.1 2.2 %collective-permute-start = (f32[16,3072]{1,0:T(8,128)}, f32[16,3072]{1,0:T(8,128)S(1)}, u32[]{:S(2)}, u32[]{:S(2)}) collective-permute-start(f32[16,3072]{1,0:T(8,128)} %get-tuple-element.14), channel_id=1, source_target_pairs={{0,4},{4,0},{8,12},{12,8},{16,20},{20,16},{24,28},{28,24},{32,36},... | collective-permute-start | bytes 589832 | tf_op jit(solution)/shard_map/ppermute | solution.py:287
  47.3 1.9 %collective-permute-start.1 = (f32[16,3072]{1,0:T(8,128)}, f32[16,3072]{1,0:T(8,128)S(1)}, u32[]{:S(2)}, u32[]{:S(2)}) collective-permute-start(f32[16,3072]{1,0:T(8,128)} %get-tuple-element.15), channel_id=1, source_target_pairs={{4,8},{8,4},{12,16},{16,12},{20,24},{24,20},{28,32},{32,28},{36,40... | collective-permute-start | bytes 589832 | tf_op jit(solution)/shard_map/ppermute | solution.py:288
  49.2 0.0 collective-permute-done.message_one
  49.2 5.8 %collective-permute-done.1.message_two = f32[16,3072]{1,0:T(8,128)S(1)} collective-permute-done((f32[16,3072]{1,0:T(8,128)}, f32[16,3072]{1,0:T(8,128)S(1)}, u32[]{:S(2)}, u32[]{:S(2)}) %collective-permute-start.1) | collective-permute-done | bytes 196640 | tf_op jit(solution)/shard_map/ppermute | solution.py:288
  55.0 0.0 copy-start.5
  55.0 0.7 %copy-done.5 = f32[16,3072]{1,0:T(8,128)} copy-done((f32[16,3072]{1,0:T(8,128)}, f32[16,3072]{1,0:T(8,128)S(1)}, u32[]{:S(2)}) %copy-start.5) | copy-done | bytes 196632
  55.7 2.1 %all-to-all-done.2 = f32[256,1,128]{2,1,0:T(1,128)S(1)} async-done(((f32[256,1,128]{2,1,0:T(1,128)}), f32[256,1,128]{2,1,0:T(1,128)S(1)}, u32[]{:S(2)}, u32[]{:S(2)}) %all-to-all-start.2) | async-done | bytes 131104 | tf_op jit(solution)/shard_map/all_to_all | solution.py:309
  57.8 0.0 copy-done
  57.8 0.0 copy-done.1
  57.8 0.0 copy-done.8
  57.8 0.0 copy-done.9
  57.8 0.0 copy-start.2
  57.8 1.7 %copy-done.2 = f32[3,64,3072]{2,1,0:T(8,128)S(1)} copy-done((f32[3,64,3072]{2,1,0:T(8,128)S(1)}, f32[3,64,3072]{2,1,0:T(8,128)}, u32[]{:S(2)}) %copy-start.2) | copy-done | bytes 2359320
  59.5 0.0 copy-start.3
  59.5 1.1 %copy-done.3 = f32[4,3,64,256]{3,2,1,0:T(8,128)S(1)} copy-done((f32[4,3,64,256]{3,2,1,0:T(8,128)S(1)}, f32[4,3,64,256]{3,2,1,0:T(8,128)}, u32[]{:S(2)}) %copy-start.3) | copy-done | bytes 786456
  60.6 0.0 copy-start.4
  60.6 1.1 %copy-done.4 = f32[64,3072]{1,0:T(8,128)S(1)} copy-done((f32[64,3072]{1,0:T(8,128)S(1)}, f32[64,3072]{1,0:T(8,128)}, u32[]{:S(2)}) %copy-start.4) | copy-done | bytes 786456
  61.8 0.0 copy-start.6
  61.8 0.9 %copy-done.6 = f32[16,3072]{1,0:T(8,128)S(1)} copy-done((f32[16,3072]{1,0:T(8,128)S(1)}, f32[16,3072]{1,0:T(8,128)}, u32[]{:S(2)}) %copy-start.6) | copy-done | bytes 196632
  62.7 0.0 copy-start.7
  62.7 0.7 %copy-done.7 = f32[1,3072]{1,0:T(1,128)S(1)} copy-done((f32[1,3072]{1,0:T(1,128)S(1)}, f32[1,3072]{1,0:T(1,128)}, u32[]{:S(2)}) %copy-start.7) | copy-done | bytes 12312
  63.4 4.1 %update.1 = (f32[3,64,3072]{2,1,0:T(8,128)}, f32[3,64,3072]{2,1,0:T(8,128)}) custom-call(s32[1]{0:T(128)} %bitcast.where, f32[3,64,3072]{2,1,0:T(8,128)S(1)} %copy-done, f32[3,64,3072]{2,1,0:T(8,128)S(1)} %copy-done.2, f32[64,3072]{1,0:T(8,128)S(1)} %copy-done.1, f32[64,3072]{1,0:T(8,128)S(1)} %copy-done.4, f32[1,3072]{1,0:T(1,128)S(1)} %copy-done.7, ...), custom_call_target="tpu_custom_call" | custom-call | tf_op jit(solution)/shard_map/update/pallas_call | solution.py:311
  (1 shorter events, 0.0 us)
Async XLA Ops:
  0.7 57.1 %copy-start = (f32[3,64,3072]{2,1,0:T(8,128)S(1)}, f32[3,64,3072]{2,1,0:T(8,128)}, u32[]{:S(2)}) copy-start(f32[3,64,3072]{2,1,0:T(8,128)} %fields.3) | copy-start | bytes 7077892
  0.7 57.1 %copy-start.1 = (f32[64,3072]{1,0:T(8,128)S(1)}, f32[64,3072]{1,0:T(8,128)}, u32[]{:S(2)}) copy-start(f32[64,3072]{1,0:T(8,128)} %source.5) | copy-start | bytes 2359300
  0.7 57.1 %copy-start.8 = (f32[64]{0:T(128)S(1)}, f32[64]{0:T(128)}, u32[]{:S(2)}) copy-start(f32[64]{0:T(128)} %param.11) | copy-start | bytes 772
  0.7 57.1 %copy-start.9 = (f32[64]{0:T(128)S(1)}, f32[64]{0:T(128)}, u32[]{:S(2)}) copy-start(f32[64]{0:T(128)} %param.12) | copy-start | bytes 772
  16.5 15.8 %copy-start.10 = (f32[8,24,128]{2,1,0:T(8,128)}, f32[8,24,128]{2,1,0:T(8,128)S(1)}, u32[]{:S(2)}) copy-start(f32[8,24,128]{2,1,0:T(8,128)S(1)} %all_to_all.21.inner) | copy-start | bytes 294916
  17.2 15.2 %all-to-all-start.1 = ((f32[8,24,128]{2,1,0:T(8,128)}), f32[8,24,128]{2,1,0:T(8,128)S(1)}, u32[]{:S(2)}, u32[]{:S(2)}) async-start(f32[8,24,128]{2,1,0:T(8,128)} %broadcast_in_dim.13), calls=%async_computation.1 | async-start | bytes 196608 | tf_op jit(solution)/shard_map/all_to_all | solution.py:292
  32.3 0.6 copy-start.11
  37.2 20.6 %all-to-all-start.2 = ((f32[256,1,128]{2,1,0:T(1,128)}), f32[256,1,128]{2,1,0:T(1,128)S(1)}, u32[]{:S(2)}, u32[]{:S(2)}) async-start(f32[256,1,128]{2,1,0:T(1,128)} %bitcast.14), calls=%async_computation.2 | async-start | bytes 262144 | tf_op jit(solution)/shard_map/all_to_all | solution.py:309
  45.1 4.2 %collective-permute-start = (f32[16,3072]{1,0:T(8,128)}, f32[16,3072]{1,0:T(8,128)S(1)}, u32[]{:S(2)}, u32[]{:S(2)}) collective-permute-start(f32[16,3072]{1,0:T(8,128)} %get-tuple-element.14), channel_id=1, source_target_pairs={{0,4},{4,0},{8,12},{12,8},{16,20},{20,16},{24,28},{28,24},{32,36},... | collective-permute-start | bytes 589832 | tf_op jit(solution)/shard_map/ppermute | solution.py:287
  47.3 7.7 %collective-permute-start.1 = (f32[16,3072]{1,0:T(8,128)}, f32[16,3072]{1,0:T(8,128)S(1)}, u32[]{:S(2)}, u32[]{:S(2)}) collective-permute-start(f32[16,3072]{1,0:T(8,128)} %get-tuple-element.15), channel_id=1, source_target_pairs={{4,8},{8,4},{12,16},{16,12},{20,24},{24,20},{28,32},{32,28},{36,40... | collective-permute-start | bytes 589832 | tf_op jit(solution)/shard_map/ppermute | solution.py:288
  55.0 0.7 %copy-start.5 = (f32[16,3072]{1,0:T(8,128)}, f32[16,3072]{1,0:T(8,128)S(1)}, u32[]{:S(2)}) copy-start(f32[16,3072]{1,0:T(8,128)S(1)} %collective-permute-done.1.message_two) | copy-start | bytes 589828
  57.8 1.7 %copy-start.2 = (f32[3,64,3072]{2,1,0:T(8,128)S(1)}, f32[3,64,3072]{2,1,0:T(8,128)}, u32[]{:S(2)}) copy-start(f32[3,64,3072]{2,1,0:T(8,128)} %register.1) | copy-start | bytes 7077892
  59.5 1.1 %copy-start.3 = (f32[4,3,64,256]{3,2,1,0:T(8,128)S(1)}, f32[4,3,64,256]{3,2,1,0:T(8,128)}, u32[]{:S(2)}) copy-start(f32[4,3,64,256]{3,2,1,0:T(8,128)} %constant.41.clone.table) | copy-start | bytes 2359300
  60.6 1.1 %copy-start.4 = (f32[64,3072]{1,0:T(8,128)S(1)}, f32[64,3072]{1,0:T(8,128)}, u32[]{:S(2)}) copy-start(f32[64,3072]{1,0:T(8,128)} %get-tuple-element.10.velocity) | copy-start | bytes 2359300
  61.8 0.9 %copy-start.6 = (f32[16,3072]{1,0:T(8,128)S(1)}, f32[16,3072]{1,0:T(8,128)}, u32[]{:S(2)}) copy-start(f32[16,3072]{1,0:T(8,128)} %copy-done.5) | copy-start | bytes 589828
  62.7 0.7 %copy-start.7 = (f32[1,3072]{1,0:T(1,128)S(1)}, f32[1,3072]{1,0:T(1,128)}, u32[]{:S(2)}) copy-start(f32[1,3072]{1,0:T(1,128)} %get-tuple-element.13.offset) | copy-start | bytes 36868

commit v2 on v1

v2 whole, which is shorter than its diff:
```python
import functools

import jax
import jax.numpy as jnp
import numpy as np
from jax import lax
from jax.experimental import pallas as pl
from jax.experimental.pallas import tpu as pltpu
from jax.sharding import Mesh
from jax.sharding import PartitionSpec as P

ALPHA_ONE = 1.0 / 3.0
COEF_ONE = 14.0 / 9.0
WIDE_ONE = 1.0 / 9.0
ALPHA_TWO = 2.0 / 11.0
COEF_TWO = 12.0 / 11.0
WIDE_TWO = 3.0 / 11.0
VISCOSITY = 0.25
DIFFUSIVITY = 0.2
COURANT = 1.2
KEEP_FACTOR = -5.0 / 9.0
STEP_FACTOR = 15.0 / 16.0

LANES = 128
CHUNK = 1024
GRANT = 24 * 1024 * 1024
MESSAGE = 16
DEPTH = 256


def inverse(alpha, length):
    matrix = np.eye(length) + alpha * (np.eye(length, k=1) + np.eye(length, k=-1))
    return np.linalg.inv(matrix)


@functools.cache
def operators(cells):
    length = 4 * cells
    near_up, near_down = np.eye(length, k=1), np.eye(length, k=-1)
    far_up, far_down = np.eye(length, k=2), np.eye(length, k=-2)
    first = COEF_ONE / 2.0 * (near_up - near_down) + WIDE_ONE / 4.0 * (far_up - far_down)
    second = COEF_TWO * (near_up - 2.0 * np.eye(length) + near_down) + WIDE_TWO / 4.0 * (
        far_up - 2.0 * np.eye(length) + far_down
    )
    slope = inverse(ALPHA_ONE, length) @ first
    bend = inverse(ALPHA_TWO, length) @ second
    integral = -(np.tril(np.ones((length, length))) - 0.5 * np.eye(length))
    constant = slope @ np.ones(length)
    return slope, bend, slope @ integral, constant


def from_left(matrix, block, cells):
    start = block * cells
    part = matrix[start : start + cells, start - cells : start]
    weights = part[1]
    factors = part[:, cells - 2] / part[1, cells - 2]
    corner = np.zeros(cells)
    corner[0] = part[0, cells - 1] - factors[0] * part[1, cells - 1]
    return factors, weights, corner


def from_right(matrix, block, cells):
    start = block * cells
    part = matrix[start : start + cells, start + cells : start + 2 * cells]
    weights = part[cells - 2]
    factors = part[:, 1] / part[cells - 2, 1]
    corner = np.zeros(cells)
    corner[cells - 1] = part[cells - 1, 0] - factors[cells - 1] * part[cells - 2, 0]
    return factors, weights, corner


@functools.cache
def tables(cells):
    slope, bend, drift, constant = operators(cells)
    kinds = (0, 2, 1, 3)
    send = np.zeros((4, cells, LANES))
    solve = np.zeros((4, 3, cells, DEPTH))
    for kind, block in enumerate(kinds):
        odd = kind >= 2
        start = block * cells
        own = slice(start, start + cells)
        rest = np.zeros(4 * cells)
        if block == 3:
            rest[own] = constant[own]
        local = drift + rest[:, None] * (np.arange(4 * cells) < start)[None, :]
        for which, matrix in enumerate((slope, bend, local)):
            base = np.zeros((cells, cells + 8))
            base[:, :cells] = matrix[own, own]
            left, right = (0, 4) if odd else (4, 0)
            slot = 1 if which == 1 else 0
            if block > 0:
                factors, _, corner = from_left(matrix, block, cells)
                base[:, cells + left + slot] = factors
                base[:, cells + left + 2] = corner
            if block < 3:
                factors, _, corner = from_right(matrix, block, cells)
                base[:, cells + right + slot] = factors
                base[:, cells + right + 2] = corner
            if which == 2:
                base[:, cells + 1] = -rest[own]
            for copy in range(3):
                solve[kind, which, :, copy * cells : (copy + 1) * cells] = base[:, :cells]
                solve[kind, which, :, 3 * cells + 8 * copy : 3 * cells + 8 * copy + 8] = base[:, cells:]
            to_right = to_left = np.zeros(cells)
            sent = (slope, bend, drift)[which]
            if block < 2:
                to_right = from_left(sent, block + 1, cells)[1]
            elif block == 2:
                to_right = from_left(sent, 2, cells)[1]
            if block > 0:
                to_left = from_right(sent, block - 1, cells)[1]
            pair = (to_left, to_right) if odd else (to_right, to_left)
            send[kind, :, which] = pair[0]
            send[kind, :, 3 + which] = pair[1]
    return send.astype(np.float32), solve.astype(np.float32)


def column(row):
    size = row.shape[1]
    rows = lax.broadcasted_iota(jnp.int32, (size, size), 0)
    columns = lax.broadcasted_iota(jnp.int32, (size, size), 1)
    spread = jnp.broadcast_to(row, (size, size))
    return jnp.sum(jnp.where(rows == columns, spread, 0.0), axis=1, keepdims=True)


def halves(value):
    high = value.astype(jnp.bfloat16)
    low = (value - high.astype(jnp.float32)).astype(jnp.bfloat16)
    return high, low


def pieces_of(lines):
    return [slice(start, start + CHUNK) for start in range(0, lines, CHUNK)]


def totals_kernel(source, metric, totals, held, held_metric, sems):
    pieces = pieces_of(source.shape[1])
    metric_copy = pltpu.make_async_copy(metric, held_metric, sems.at[len(pieces)])
    metric_copy.start()
    copies = [pltpu.make_async_copy(source.at[:, p], held.at[:, p], sems.at[i]) for i, p in enumerate(pieces)]
    for copy in copies:
        copy.start()
    metric_copy.wait()
    scale = 1.0 / column(held_metric[...])
    for i, p in enumerate(pieces):
        copies[i].wait()
        total = jnp.sum(held[:, p] * scale, axis=0, keepdims=True)
        for peer in range(totals.shape[0]):
            for k in range(CHUNK // LANES):
                row = i * (CHUNK // LANES) + k
                totals[peer, row : row + 1, :] = total[:, k * LANES : (k + 1) * LANES]


def send_kernel(
    kind, fields, source, metric, weights, message_one, message_two, held, held_source, held_metric, held_weights, sems
):
    cells, lines = source.shape
    pieces = pieces_of(lines)
    metric_copy = pltpu.make_async_copy(metric, held_metric, sems.at[2, 0])
    metric_copy.start()
    weights_copy = pltpu.make_async_copy(weights.at[kind[0]], held_weights, sems.at[2, 1])
    weights_copy.start()
    copies = []
    for i, p in enumerate(pieces):
        pair = (
            pltpu.make_async_copy(fields.at[:, :, p], held.at[:, :, p], sems.at[0, i]),
            pltpu.make_async_copy(source.at[:, p], held_source.at[:, p], sems.at[1, i]),
        )
        for copy in pair:
            copy.start()
        copies.append(pair)
    odd = kind[0] >= 2
    metric_copy.wait()
    weights_copy.wait()
    chosen = held_weights[...]
    scale = 1.0 / column(held_metric[...])
    blank = jnp.zeros((1, CHUNK), jnp.float32)
    for i, p in enumerate(pieces):
        for copy in copies[i]:
            copy.wait()
        for k in range(4):
            value = held[k, :, p] if k < 3 else held_source[:, p] * scale
            first, last = value[:1], value[cells - 1 :]
            for message, begin in ((message_one, 0), (message_two, 3)):
                row = 4 * k
                if k < 3:
                    for which in range(2):
                        weight = chosen[:, begin + which : begin + which + 1]
                        message[row + which : row + which + 1, p] = jnp.sum(value * weight, axis=0, keepdims=True)
                else:
                    weight = chosen[:, begin + 2 : begin + 3]
                    message[row : row + 1, p] = jnp.sum(value * weight, axis=0, keepdims=True)
                    message[row + 1 : row + 2, p] = blank
                edge = jnp.where(odd, first, last) if begin == 0 else jnp.where(odd, last, first)
                message[row + 2 : row + 3, p] = edge
                message[row + 3 : row + 4, p] = blank


def slab_kernel(inner, after_one, after_two, sums):
    del after_one, after_two
    total = inner[0]
    for peer in range(1, inner.shape[0]):
        total += inner[peer]
    for peer in range(sums.shape[0]):
        sums[peer] = total


def running_kernel(after, source, metric, lower, running, spread, held, held_metric, sems):
    del after
    pieces = pieces_of(source.shape[1])
    metric_copy = pltpu.make_async_copy(metric, held_metric, sems.at[len(pieces)])
    metric_copy.start()
    copies = [pltpu.make_async_copy(source.at[:, p], held.at[:, p], sems.at[i]) for i, p in enumerate(pieces)]
    for copy in copies:
        copy.start()
    metric_copy.wait()
    stretch = column(held_metric[...])
    spread[...] = jnp.broadcast_to(stretch, spread.shape)
    scale = 1.0 / stretch
    for i, p in enumerate(pieces):
        copies[i].wait()
        scaled = held[:, p] * scale
        high = scaled.astype(jnp.bfloat16)
        rest = scaled - high.astype(jnp.float32)
        middle = rest.astype(jnp.bfloat16)
        low = (rest - middle.astype(jnp.float32)).astype(jnp.bfloat16)
        stacked = jnp.concatenate([high, middle, low], axis=0)
        running[:, p] = jnp.dot(lower[...], stacked, preferred_element_type=jnp.float32)


def velocity_kernel(place, slab, running, spread, inner, outer, velocity, offset, rate):
    stretch = spread[...]
    squared = 4.0 * VISCOSITY * stretch * stretch
    before = jnp.zeros(inner.shape[1:], jnp.float32)
    for peer in range(inner.shape[0]):
        before += jnp.where(peer < place[0], inner[peer], 0.0)
    for peer in range(outer.shape[0]):
        before += jnp.where(peer < slab[0], outer[peer], 0.0)
    top = jnp.zeros((1, LANES), jnp.float32)
    for k in range(before.shape[0]):
        here = slice(k * LANES, (k + 1) * LANES)
        shift = before[k : k + 1, :]
        offset[:, here] = shift
        value = -(running[:, here] + shift)
        velocity[:, here] = value
        top = jnp.maximum(top, jnp.max(jnp.abs(value) * stretch + squared, axis=0, keepdims=True))
    peak = jnp.max(top, axis=1, keepdims=True)
    rate[...] = jnp.broadcast_to(peak, rate.shape)


def tendency_kernel(
    kind, fields, source, velocity, offset, spread, message_one, message_two, curvature, table,
    tendency, velocity_out,
    held_fields, held_source, held_table, held_curvature, mixed, mixed_scalar, drift, sems,
):
    cells, lines = source.shape
    pieces = pieces_of(lines)
    table_copy = pltpu.make_async_copy(table.at[kind[0]], held_table, sems.at[2, 0])
    table_copy.start()
    curvature_copy = pltpu.make_async_copy(curvature, held_curvature, sems.at[2, 1])
    curvature_copy.start()
    copies = []
    for i, p in enumerate(pieces):
        group = (
            pltpu.make_async_copy(source.at[:, p], held_source.at[:, p], sems.at[0, i]),
            pltpu.make_async_copy(fields.at[:, :, p], held_fields.at[:, :, p], sems.at[1, i]),
        )
        for copy in group:
            copy.start()
        copies.append(group)
    out_copy = pltpu.make_async_copy(velocity, velocity_out, sems.at[2, 2])
    out_copy.start()

    stretch = spread[:, :1]
    table_copy.wait()
    curvature_copy.wait()
    curving = column(held_curvature[...])
    slope, bend = held_table[0], held_table[1]
    lane = lax.broadcasted_iota(jnp.int32, (cells, DEPTH), 1)
    is_low = ((lane >= 2 * cells) & (lane < 3 * cells)) | (lane >= 3 * cells + 16)

    def split(value):
        high, low = halves(value)
        return jnp.where(is_low, low.astype(jnp.float32), high.astype(jnp.float32)).astype(jnp.bfloat16)

    field_x = stretch * slope
    field_xx = stretch * stretch * bend + curving * slope
    mixed[:cells, :] = split(field_x)
    mixed[cells:, :] = split(VISCOSITY * field_xx)
    mixed_scalar[:cells, :] = mixed[:cells, :]
    mixed_scalar[cells:, :] = split(DIFFUSIVITY * field_xx)
    drift[...] = split(stretch * held_table[2])

    def stacked(value, tail):
        high, low = halves(value)
        tail_high = tail.astype(jnp.bfloat16).astype(jnp.float32)
        tail_low = tail - tail_high
        tails = jnp.concatenate(
            [tail_high, tail_low, tail_high, jnp.zeros((DEPTH - 3 * cells - 24, CHUNK), jnp.float32)], axis=0
        ).astype(jnp.bfloat16)
        return jnp.concatenate([high, low, high, tails], axis=0)

    for i, p in enumerate(pieces):
        copies[i][0].wait()
        scaled = held_source[:, p] * (1.0 / stretch)
        lead = message_one[12:16, p]
        row = lax.broadcasted_iota(jnp.int32, lead.shape, 0)
        lead = jnp.where(row == 1, offset[:, p], lead)
        tail = jnp.concatenate([lead, message_two[12:16, p]], axis=0)
        velocity_x = jnp.dot(drift[...], stacked(scaled, tail), preferred_element_type=jnp.float32)
        speed = velocity[:, p]
        copies[i][1].wait()
        for k in range(3):
            field = held_fields[k, :, p]
            tail = jnp.concatenate([message_one[4 * k : 4 * k + 4, p], message_two[4 * k : 4 * k + 4, p]], axis=0)
            weights = mixed if k < 2 else mixed_scalar
            both = jnp.dot(weights[...], stacked(field, tail), preferred_element_type=jnp.float32)
            tendency[k, :, p] = both[cells:] - (speed * both[:cells] + field * velocity_x)
    out_copy.wait()


def update_kernel(fields, register, tendency, rates, new_fields, new_register, held_fields, held_register, sems):
    pieces = [(k, p) for k in range(3) for p in pieces_of(tendency.shape[2])]
    arrivals = []
    for i, (k, p) in enumerate(pieces):
        pair = (
            pltpu.make_async_copy(register.at[k, :, p], held_register.at[k, :, p], sems.at[0, i]),
            pltpu.make_async_copy(fields.at[k, :, p], held_fields.at[k, :, p], sems.at[1, i]),
        )
        for copy in pair:
            copy.start()
        arrivals.append(pair)
    time_step = COURANT / jnp.max(jnp.max(rates[...], axis=0, keepdims=True), axis=1, keepdims=True)
    departures = []
    for i, (k, p) in enumerate(pieces):
        arrivals[i][0].wait()
        updated = KEEP_FACTOR * held_register[k, :, p] + time_step * tendency[k, :, p]
        held_register[k, :, p] = updated
        departures.append(pltpu.make_async_copy(held_register.at[k, :, p], new_register.at[k, :, p], sems.at[2, i]))
        departures[-1].start()
        arrivals[i][1].wait()
        held_fields[k, :, p] = held_fields[k, :, p] + STEP_FACTOR * updated
        departures.append(pltpu.make_async_copy(held_fields.at[k, :, p], new_fields.at[k, :, p], sems.at[3, i]))
        departures[-1].start()
    for copy in departures:
        copy.wait()


def local(fields, register, source, metric, curvature):
    cells, lines = source.shape
    steps = lines // CHUNK
    groups = lines // LANES
    inner_count, slab_count = lax.axis_size("inner"), lax.axis_size("slab")
    count = inner_count * slab_count
    devices = count * lax.axis_size("gz")
    inner, slab = lax.axis_index("inner"), lax.axis_index("slab")
    position = slab * inner_count + inner
    kind = jnp.where(position == 0, 0, jnp.where(position == count - 1, 3, 1 + position % 2))
    kind, inner, slab = (jnp.reshape(value, (1,)).astype(jnp.int32) for value in (kind, inner, slab))
    send_weights, solve_tables = tables(cells)
    metric_row, curvature_row = metric[None, :], curvature[None, :]

    smem = pl.BlockSpec(memory_space=pltpu.SMEM)
    vmem = pl.BlockSpec(memory_space=pltpu.VMEM)
    hbm = pl.BlockSpec(memory_space=pl.ANY)

    def shape(*sizes):
        return jax.ShapeDtypeStruct(sizes, jnp.float32)

    def fast(*sizes):
        return pltpu.VMEM(sizes, jnp.float32)

    def keep(value):
        return pltpu.with_memory_space_constraint(value, pltpu.VMEM)

    def far(value):
        return pltpu.with_memory_space_constraint(value, pltpu.HBM)

    def cost(bytes_accessed, flops=0):
        return pl.CostEstimate(flops=flops, bytes_accessed=bytes_accessed, transcendentals=0)

    params = pltpu.CompilerParams(vmem_limit_bytes=GRANT)
    line_bytes = 4 * cells * lines
    source, fields, register = far(source), far(fields), far(register)
    metric_row, curvature_row = far(metric_row), far(curvature_row)
    semaphores = pltpu.SemaphoreType.DMA
    one_row = fast(1, cells)

    totals = pl.pallas_call(
        totals_kernel,
        in_specs=[hbm, hbm],
        out_specs=vmem,
        out_shape=fast(inner_count, groups, LANES),
        scratch_shapes=[fast(cells, lines), one_row, semaphores((steps + 1,))],
        compiler_params=params,
        cost_estimate=cost(line_bytes),
        name="totals",
    )(source, metric_row)
    inner_totals = lax.all_to_all(totals, "inner", 0, 0)

    message_one, message_two = pl.pallas_call(
        send_kernel,
        in_specs=[smem, hbm, hbm, hbm, hbm],
        out_specs=[vmem, vmem],
        out_shape=[fast(MESSAGE, lines), fast(MESSAGE, lines)],
        scratch_shapes=[fast(3, cells, lines), fast(cells, lines), one_row, fast(cells, LANES), semaphores((3, max(steps, 2)))],
        compiler_params=params,
        cost_estimate=cost(4 * line_bytes),
        name="send",
    )(kind, fields, source, metric_row, far(jnp.asarray(send_weights)))

    slab_sums = pl.pallas_call(
        slab_kernel,
        in_specs=[vmem, hbm, hbm],
        out_specs=vmem,
        out_shape=fast(slab_count, groups, LANES),
        compiler_params=params,
        name="slab",
    )(keep(inner_totals), message_one, message_two)
    slab_totals = lax.all_to_all(slab_sums, "slab", 0, 0)

    line = ("slab", "inner")
    even_pairs = [(i, i ^ 1) for i in range(count)]
    odd_pairs = [(i, i + 1 if i % 2 else i - 1) for i in range(1, count - 1)]
    got_one = lax.ppermute(message_one, line, even_pairs)
    got_two = lax.ppermute(message_two, line, odd_pairs)

    lower = np.tril(np.ones((cells, cells))) - 0.5 * np.eye(cells)
    lower = jnp.asarray(np.concatenate([lower] * 3, axis=1), jnp.bfloat16)
    running, spread = pl.pallas_call(
        running_kernel,
        in_specs=[hbm, hbm, hbm, vmem],
        out_specs=[vmem, vmem],
        out_shape=[fast(cells, lines), fast(cells, LANES)],
        scratch_shapes=[fast(cells, lines), one_row, semaphores((steps + 1,))],
        compiler_params=params,
        cost_estimate=cost(2 * line_bytes),
        name="running",
    )(slab_sums, source, metric_row, lower)

    velocity, offset, rate = pl.pallas_call(
        velocity_kernel,
        in_specs=[smem, smem, vmem, vmem, vmem, vmem],
        out_specs=[vmem, vmem, vmem],
        out_shape=[fast(cells, lines), fast(1, lines), fast(devices, LANES)],
        compiler_params=params,
        cost_estimate=cost(2 * line_bytes),
        name="velocity",
    )(inner, slab, keep(running), keep(spread), keep(inner_totals), keep(slab_totals))

    rates = lax.all_to_all(rate, ("slab", "inner", "gz"), 0, 0, tiled=True)

    tendency, velocity_out = pl.pallas_call(
        tendency_kernel,
        in_specs=[smem, hbm, hbm, vmem, vmem, vmem, vmem, vmem, hbm, hbm],
        out_specs=[vmem, hbm],
        out_shape=[fast(3, cells, lines), pltpu.HBM((cells, lines), jnp.float32)],
        scratch_shapes=[
            fast(3, cells, lines),
            fast(cells, lines),
            fast(3, cells, DEPTH),
            one_row,
            pltpu.VMEM((2 * cells, DEPTH), jnp.bfloat16),
            pltpu.VMEM((2 * cells, DEPTH), jnp.bfloat16),
            pltpu.VMEM((cells, DEPTH), jnp.bfloat16),
            semaphores((3, max(steps, 3))),
        ],
        compiler_params=params,
        cost_estimate=cost(12 * line_bytes),
        name="tendency",
    )(
        kind, fields, source, keep(velocity), keep(offset), keep(spread), got_one, got_two, curvature_row,
        far(jnp.asarray(solve_tables)),
    )

    new_fields, new_register = pl.pallas_call(
        update_kernel,
        in_specs=[hbm, hbm, vmem, vmem],
        out_specs=[hbm, hbm],
        out_shape=[pltpu.HBM((3, cells, lines), jnp.float32)] * 2,
        scratch_shapes=[fast(3, cells, lines), fast(3, cells, lines), semaphores((4, 3 * steps))],
        compiler_params=params,
        cost_estimate=cost(12 * line_bytes),
        name="update",
    )(fields, register, keep(tendency), rates)
    return (new_fields, new_register, velocity_out)


def solution(mesh):
    along, across = mesh.devices.shape
    inner = 1
    while inner * inner < along:
        inner *= 2
    split = Mesh(mesh.devices.reshape(along // inner, inner, across), ("slab", "inner", "gz"))
    line = ("slab", "inner")
    placed = (P(None, line, "gz"), P(None, line, "gz"), P(line, "gz"), P(line), P(line))
    return jax.shard_map(
        local,
        mesh=split,
        in_specs=placed,
        out_specs=(P(None, line, "gz"), P(None, line, "gz"), P(line, "gz")),
        check_vma=False,
    )
```

time: 68 us -> 56.6 us (0.83)
  blocking collectives: 11.5 us -> 0 us
  local copies, waits for them, and re-layouts: 7.55 us -> 0.01 us
  starting transfers between devices: 19.4 us -> 25.9 us
  Pallas kernels: 12.7 us -> 15.5 us
  waiting for transfers between devices: 14.9 us -> 14 us
    all_to_all x1 -> x0, blocking collectives: 11.5 us -> none  [local(): inner_totals = lax.all_to_all(totals, 'inner', 0, 0)]
    unnamed x24 -> x2, local copies, waits for them, and re-layouts: 6.9 us -> 0.01 us
    all_to_all x1 -> x2, starting transfers between devices: 7.48 us -> 14 us  [the longest x1 7.46 us: local(): slab_totals = lax.all_to_all(slab_sums, 'slab', 0, 0)]
    pallas_call x3 -> x7, Pallas kernels: 12.7 us -> 15.5 us  [the longest x1 4.42 us: local(): pl.pallas_call(update_kernel, in_specs=[hbm, hbm, vmem, vmem], out_specs=...]
    all_to_all x1, waiting for transfers between devices: 2.12 us -> 0.01 us  [local(): rates = lax.all_to_all(rate, ('slab', 'inner', 'gz'), 0, 0, tiled=True)]
    all_to_all x1 -> x2, waiting for transfers between devices: 7.04 us -> 8.41 us  [the longest x1 6.06 us: local(): slab_totals = lax.all_to_all(slab_sums, 'slab', 0, 0)]
  transfers between devices with their start and end apart: 4 -> 5, of which waited for: 3 -> 3; matrix products, arithmetic and copies ran while one was open for 1% -> 0% of each run, Pallas kernels for 0% -> 9%
where the time goes in v2:
time: 56.6 us; the launch traced here: 56.2 us
  starting transfers between devices  25.9 us (46%)
  Pallas kernels  15.5 us (27%)
  waiting for transfers between devices  14 us (25%)
  between operations  0.71 us (1%)
    all_to_all x1, starting transfers between devices, local(): rates = lax.all_to_all(rate, ('slab', 'inner', 'gz'), 0, 0, tiled=True)  7.82 us
    all_to_all x1, starting transfers between devices, local(): slab_totals = lax.all_to_all(slab_sums, 'slab', 0, 0)  7.46 us
    all_to_all x1, starting transfers between devices, local(): inner_totals = lax.all_to_all(totals, 'inner', 0, 0)  6.52 us
    all_to_all x1, waiting for transfers between devices, local(): slab_totals = lax.all_to_all(slab_sums, 'slab', 0, 0)  6.06 us
    ppermute x1, waiting for transfers between devices, local(): got_two = lax.ppermute(message_two, line, odd_pairs)  5.59 us
    pallas_call x1, Pallas kernels, local(): pl.pallas_call(update_kernel, in_specs=[hbm, hbm, vmem, vmem], out_specs=...  4.42 us
    pallas_call x1, Pallas kernels, local(): pl.pallas_call(tendency_kernel, in_specs=[smem, hbm, hbm, vmem, vmem, vme...  3.38 us
    pallas_call x1, Pallas kernels, local(): pl.pallas_call(send_kernel, in_specs=[smem, hbm, hbm, hbm, hbm], out_spec...  2.65 us
  transfers between devices with their start and end apart: 5, of which 3 were waited for; matrix products, arithmetic and copies ran while one was open for 0% of the time, Pallas kernels for 9%

profile of v2, /device:TPU:1, one launch (start us, length us, event | category | flops | bytes accessed | tf_op | source)
XLA Modules:
  0.0 56.2 jit_solution(13282595595929119952)
XLA Ops:
  0.6 1.8 %totals.1 = f32[8,24,128]{2,1,0:T(8,128)} custom-call(f32[64,3072]{1,0:T(8,128)} %source.7, f32[1,64]{1,0:T(1,128)} %bitcast.10), custom_call_target="tpu_custom_call" | custom-call | bytes 786432 | tf_op jit(solution)/shard_map/totals/pallas_call | solution.py:389
  2.5 0.0 copy-start
  2.5 6.5 %all-to-all-start = ((f32[8,24,128]{2,1,0:T(8,128)}), f32[8,24,128]{2,1,0:T(8,128)S(1)}, u32[]{:S(2)}, u32[]{:S(2)}) async-start(f32[8,24,128]{2,1,0:T(8,128)} %totals.1), calls=%async_computation | async-start | bytes 196608 | tf_op jit(solution)/shard_map/all_to_all | solution.py:399
  9.0 2.6 %send.1 = (f32[16,3072]{1,0:T(8,128)S(1)}, f32[16,3072]{1,0:T(8,128)S(1)}) custom-call(s32[1]{0:T(128)} %bitcast.kind, f32[3,64,3072]{2,1,0:T(8,128)} %fields.5, f32[64,3072]{1,0:T(8,128)} %source.7, f32[1,64]{1,0:T(1,128)} %bitcast.11, f32[4,64,128]{2,1,0:T(8,128)} %constant.37.clone.weights), custom_call_target="tpu_custom_call" | custom-call | bytes 3145728 | tf_op jit(solution)/shard_map/send/pallas_call | solution.py:401
  11.7 2.3 %all-to-all-done.inner = f32[8,24,128]{2,1,0:T(8,128)S(1)} async-done(((f32[8,24,128]{2,1,0:T(8,128)}), f32[8,24,128]{2,1,0:T(8,128)S(1)}, u32[]{:S(2)}, u32[]{:S(2)}) %all-to-all-start) | async-done | bytes 98336 | tf_op jit(solution)/shard_map/all_to_all | solution.py:399
  14.0 0.7 %slab.1.after = f32[8,24,128]{2,1,0:T(8,128)} custom-call(f32[8,24,128]{2,1,0:T(8,128)S(1)} %all-to-all-done.inner, f32[16,3072]{1,0:T(8,128)S(1)} %get-tuple-element.14.after_one, f32[16,3072]{1,0:T(8,128)S(1)} %get-tuple-element.15.after_two), custom_call_target="tpu_custom_call" | custom-call | tf_op jit(solution)/shard_map/slab/pallas_call | solution.py:412
  14.7 7.5 %all-to-all-start.1 = ((f32[8,24,128]{2,1,0:T(8,128)}), f32[8,24,128]{2,1,0:T(8,128)S(1)}, u32[]{:S(2)}, u32[]{:S(2)}) async-start(f32[8,24,128]{2,1,0:T(8,128)} %slab.1.after), calls=%async_computation.1 | async-start | bytes 196608 | tf_op jit(solution)/shard_map/all_to_all | solution.py:420
  22.1 0.0 copy-done
  22.1 1.6 %running.1 = (f32[64,3072]{1,0:T(8,128)S(1)}, f32[64,128]{1,0:T(8,128)S(1)}) custom-call(f32[8,24,128]{2,1,0:T(8,128)} %slab.1.after, f32[64,3072]{1,0:T(8,128)} %source.7, f32[1,64]{1,0:T(1,128)} %bitcast.12, bf16[64,192]{1,0:T(8,128)(2,1)S(1)} %copy-done), custom_call_target="tpu_custom_call" | custom-call | bytes 1572864 | tf_op jit(solution)/shard_map/running/pallas_call | solution.py:430
  23.7 6.1 %all-to-all-done.1.outer = f32[8,24,128]{2,1,0:T(8,128)S(1)} async-done(((f32[8,24,128]{2,1,0:T(8,128)}), f32[8,24,128]{2,1,0:T(8,128)S(1)}, u32[]{:S(2)}, u32[]{:S(2)}) %all-to-all-start.1) | async-done | bytes 98336 | tf_op jit(solution)/shard_map/all_to_all | solution.py:420
  29.8 1.0 %velocity.1 = (f32[64,3072]{1,0:T(8,128)S(1)}, f32[1,3072]{1,0:T(1,128)S(1)}, f32[256,128]{1,0:T(8,128)}) custom-call(s32[1]{0:T(128)} %bitcast.1.place, s32[1]{0:T(128)} %bitcast.2.slab, f32[64,3072]{1,0:T(8,128)S(1)} %get-tuple-element.16.running, f32[64,128]{1,0:T(8,128)S(1)} %get-tuple-element.17.spread, f32[8,24,128]{2,1,0:T(8,128)S(1)} %all-to-all-done.inner, ...), custom_call_target="tpu_custom_call" | custom-call | bytes 1572864 | tf_op jit(solution)/shard_map/velocity/pallas_call | solution.py:441
  30.8 7.8 %all-to-all-start.2 = ((f32[256,1,128]{2,1,0:T(1,128)}), f32[256,1,128]{2,1,0:T(1,128)S(1)}, u32[]{:S(2)}, u32[]{:S(2)}) async-start(f32[256,1,128]{2,1,0:T(1,128)} %bitcast.6), calls=%async_computation.2 | async-start | bytes 262144 | tf_op jit(solution)/shard_map/all_to_all | solution.py:451
  38.6 2.2 %collective-permute-start = (f32[16,3072]{1,0:T(8,128)S(1)}, f32[16,3072]{1,0:T(8,128)S(1)}, u32[]{:S(2)}, u32[]{:S(2)}) collective-permute-start(f32[16,3072]{1,0:T(8,128)S(1)} %get-tuple-element.14.after_one), channel_id=1, source_target_pairs={{0,4},{4,0},{8,12},{12,8},{16,20},{20,16},{24,28},{28,24},{32,36},... | collective-permute-start | bytes 589832 | tf_op jit(solution)/shard_map/ppermute | solution.py:425
  40.8 1.9 %collective-permute-start.1 = (f32[16,3072]{1,0:T(8,128)S(1)}, f32[16,3072]{1,0:T(8,128)S(1)}, u32[]{:S(2)}, u32[]{:S(2)}) collective-permute-start(f32[16,3072]{1,0:T(8,128)S(1)} %get-tuple-element.15.after_two), channel_id=1, source_target_pairs={{4,8},{8,4},{12,16},{16,12},{20,24},{24,20},{28,32},{32,28},{36,40... | collective-permute-start | bytes 589832 | tf_op jit(solution)/shard_map/ppermute | solution.py:426
  42.7 0.0 collective-permute-done.message_one
  42.7 5.6 %collective-permute-done.1.message_two = f32[16,3072]{1,0:T(8,128)S(1)} collective-permute-done((f32[16,3072]{1,0:T(8,128)S(1)}, f32[16,3072]{1,0:T(8,128)S(1)}, u32[]{:S(2)}, u32[]{:S(2)}) %collective-permute-start.1) | collective-permute-done | bytes 196640 | tf_op jit(solution)/shard_map/ppermute | solution.py:426
  48.3 3.4 %tendency.1 = (f32[3,64,3072]{2,1,0:T(8,128)S(1)}, f32[64,3072]{1,0:T(8,128)}) custom-call(s32[1]{0:T(128)} %bitcast.kind, f32[3,64,3072]{2,1,0:T(8,128)} %fields.5, f32[64,3072]{1,0:T(8,128)} %source.7, f32[64,3072]{1,0:T(8,128)S(1)} %get-tuple-element.18.velocity, f32[1,3072]{1,0:T(1,128)S(1)} %get-tuple-element.19.offset, ...), custom_call_target="tpu_custom_call" | custom-call | bytes 9437184 | tf_op jit(solution)/shard_map/tendency/pallas_call | solution.py:453
  51.7 0.0 all-to-all-done.2
  51.7 4.4 %update.1 = (f32[3,64,3072]{2,1,0:T(8,128)}, f32[3,64,3072]{2,1,0:T(8,128)}) custom-call(f32[3,64,3072]{2,1,0:T(8,128)} %fields.5, f32[3,64,3072]{2,1,0:T(8,128)} %register.1, f32[3,64,3072]{2,1,0:T(8,128)S(1)} %get-tuple-element.20.tendency, f32[256,128]{1,0:T(8,128)S(1)} %bitcast.9), custom_call_target="tpu_custom_call" | custom-call | bytes 9437184 | tf_op jit(solution)/shard_map/update/pallas_call | solution.py:476
Async XLA Ops:
  2.5 19.7 %copy-start = (bf16[64,192]{1,0:T(8,128)(2,1)S(1)}, bf16[64,192]{1,0:T(8,128)(2,1)}, u32[]{:S(2)}) copy-start(bf16[64,192]{1,0:T(8,128)(2,1)} %constant.38.clone.lower) | copy-start | bytes 73732
  2.5 11.5 %all-to-all-start = ((f32[8,24,128]{2,1,0:T(8,128)}), f32[8,24,128]{2,1,0:T(8,128)S(1)}, u32[]{:S(2)}, u32[]{:S(2)}) async-start(f32[8,24,128]{2,1,0:T(8,128)} %totals.1), calls=%async_computation | async-start | bytes 196608 | tf_op jit(solution)/shard_map/all_to_all | solution.py:399
  14.7 15.1 %all-to-all-start.1 = ((f32[8,24,128]{2,1,0:T(8,128)}), f32[8,24,128]{2,1,0:T(8,128)S(1)}, u32[]{:S(2)}, u32[]{:S(2)}) async-start(f32[8,24,128]{2,1,0:T(8,128)} %slab.1.after), calls=%async_computation.1 | async-start | bytes 196608 | tf_op jit(solution)/shard_map/all_to_all | solution.py:420
  30.8 21.0 %all-to-all-start.2 = ((f32[256,1,128]{2,1,0:T(1,128)}), f32[256,1,128]{2,1,0:T(1,128)S(1)}, u32[]{:S(2)}, u32[]{:S(2)}) async-start(f32[256,1,128]{2,1,0:T(1,128)} %bitcast.6), calls=%async_computation.2 | async-start | bytes 262144 | tf_op jit(solution)/shard_map/all_to_all | solution.py:451
  38.6 4.2 %collective-permute-start = (f32[16,3072]{1,0:T(8,128)S(1)}, f32[16,3072]{1,0:T(8,128)S(1)}, u32[]{:S(2)}, u32[]{:S(2)}) collective-permute-start(f32[16,3072]{1,0:T(8,128)S(1)} %get-tuple-element.14.after_one), channel_id=1, source_target_pairs={{0,4},{4,0},{8,12},{12,8},{16,20},{20,16},{24,28},{28,24},{32,36},... | collective-permute-start | bytes 589832 | tf_op jit(solution)/shard_map/ppermute | solution.py:425
  40.8 7.5 %collective-permute-start.1 = (f32[16,3072]{1,0:T(8,128)S(1)}, f32[16,3072]{1,0:T(8,128)S(1)}, u32[]{:S(2)}, u32[]{:S(2)}) collective-permute-start(f32[16,3072]{1,0:T(8,128)S(1)} %get-tuple-element.15.after_two), channel_id=1, source_target_pairs={{4,8},{8,4},{12,16},{16,12},{20,24},{24,20},{28,32},{32,28},{36,40... | collective-permute-start | bytes 589832 | tf_op jit(solution)/shard_map/ppermute | solution.py:426

commit v3 on v2

--- a/solution.py
+++ b/solution.py
@@ -22,9 +22,9 @@
 STEP_FACTOR = 15.0 / 16.0
 
 LANES = 128
-CHUNK = 1024
+STEPS = 4
 GRANT = 24 * 1024 * 1024
-MESSAGE = 16
+MESSAGE = 11
 DEPTH = 256
 
 
@@ -129,42 +129,73 @@
     return high, low
 
 
-def pieces_of(lines):
-    return [slice(start, start + CHUNK) for start in range(0, lines, CHUNK)]
+def pieces_of(lines, count=STEPS):
+    width = lines // count
+    return [slice(start, start + width) for start in range(0, lines, width)]
+
+
+def message_shape(lines):
+    return 8, lines + (MESSAGE - 8) * (lines // 8)
+
+
+def put(message, row, part, value):
+    width = value.shape[1]
+    fold = width // 2
+    if row < 8:
+        message[row : row + 1, part * width : (part + 1) * width] = value
+        return
+    start = STEPS * width + (row - 8) * fold
+    for half in range(2):
+        line = 2 * part + half
+        message[line : line + 1, start : start + fold] = value[:, half * fold : (half + 1) * fold]
+
+
+def take(message, row, part, width):
+    fold = width // 2
+    if row < 8:
+        return message[row : row + 1, part * width : (part + 1) * width]
+    start = STEPS * width + (row - 8) * fold
+    return jnp.concatenate(
+        [message[2 * part + half : 2 * part + half + 1, start : start + fold] for half in range(2)], axis=1
+    )
 
 
 def totals_kernel(source, metric, totals, held, held_metric, sems):
-    pieces = pieces_of(source.shape[1])
-    metric_copy = pltpu.make_async_copy(metric, held_metric, sems.at[len(pieces)])
+    cells, lines = source.shape
+    metric_copy = pltpu.make_async_copy(metric, held_metric, sems.at[2])
     metric_copy.start()
-    copies = [pltpu.make_async_copy(source.at[:, p], held.at[:, p], sems.at[i]) for i, p in enumerate(pieces)]
+    rows = [slice(0, cells // 2), slice(cells // 2, cells)]
+    copies = [pltpu.make_async_copy(source.at[r, :], held.at[r, :], sems.at[i]) for i, r in enumerate(rows)]
     for copy in copies:
         copy.start()
     metric_copy.wait()
     scale = 1.0 / column(held_metric[...])
-    for i, p in enumerate(pieces):
-        copies[i].wait()
-        total = jnp.sum(held[:, p] * scale, axis=0, keepdims=True)
-        for peer in range(totals.shape[0]):
-            for k in range(CHUNK // LANES):
-                row = i * (CHUNK // LANES) + k
-                totals[peer, row : row + 1, :] = total[:, k * LANES : (k + 1) * LANES]
+    total = jnp.zeros((1, lines), jnp.float32)
+    for copy, r in zip(copies, rows):
+        copy.wait()
+        total += jnp.sum(held[r, :] * scale[r], axis=0, keepdims=True)
+    for peer in range(totals.shape[0]):
+        for k in range(lines // LANES):
+            totals[peer, k : k + 1, :] = total[:, k * LANES : (k + 1) * LANES]
 
 
 def send_kernel(
-    kind, fields, source, metric, weights, message_one, message_two, held, held_source, held_metric, held_weights, sems
+    kind, fields, source, metric, weights, lower, message_one, message_two, running, spread,
+    held, held_source, held_metric, held_weights, held_lower, sems,
 ):
     cells, lines = source.shape
-    pieces = pieces_of(lines)
+    pieces = pieces_of(lines, STEPS // 2)
     metric_copy = pltpu.make_async_copy(metric, held_metric, sems.at[2, 0])
     metric_copy.start()
     weights_copy = pltpu.make_async_copy(weights.at[kind[0]], held_weights, sems.at[2, 1])
     weights_copy.start()
+    lower_copy = pltpu.make_async_copy(lower, held_lower, sems.at[2, 2])
+    lower_copy.start()
     copies = []
     for i, p in enumerate(pieces):
         pair = (
+            pltpu.make_async_copy(source.at[:, p], held_source.at[:, p], sems.at[1, i]),
             pltpu.make_async_copy(fields.at[:, :, p], held.at[:, :, p], sems.at[0, i]),
-            pltpu.make_async_copy(source.at[:, p], held_source.at[:, p], sems.at[1, i]),
         )
         for copy in pair:
             copy.start()
@@ -172,28 +203,33 @@
     odd = kind[0] >= 2
     metric_copy.wait()
     weights_copy.wait()
+    lower_copy.wait()
     chosen = held_weights[...]
-    scale = 1.0 / column(held_metric[...])
-    blank = jnp.zeros((1, CHUNK), jnp.float32)
-    for i, p in enumerate(pieces):
-        for copy in copies[i]:
-            copy.wait()
+    stretch = column(held_metric[...])
+    spread[...] = jnp.broadcast_to(stretch, spread.shape)
+    scale = 1.0 / stretch
+    for i, p in enumerate(pieces_of(lines)):
+        if i % 2 == 0:
+            for copy in copies[i // 2]:
+                copy.wait()
+        scaled = held_source[:, p] * scale
+        high = scaled.astype(jnp.bfloat16)
+        rest = scaled - high.astype(jnp.float32)
+        middle = rest.astype(jnp.bfloat16)
+        low = (rest - middle.astype(jnp.float32)).astype(jnp.bfloat16)
+        running[:, p] = jnp.dot(
+            held_lower[...], jnp.concatenate([high, middle, low], axis=0), preferred_element_type=jnp.float32
+        )
         for k in range(4):
-            value = held[k, :, p] if k < 3 else held_source[:, p] * scale
+            value = held[k, :, p] if k < 3 else scaled
             first, last = value[:1], value[cells - 1 :]
             for message, begin in ((message_one, 0), (message_two, 3)):
-                row = 4 * k
-                if k < 3:
-                    for which in range(2):
-                        weight = chosen[:, begin + which : begin + which + 1]
-                        message[row + which : row + which + 1, p] = jnp.sum(value * weight, axis=0, keepdims=True)
-                else:
-                    weight = chosen[:, begin + 2 : begin + 3]
-                    message[row : row + 1, p] = jnp.sum(value * weight, axis=0, keepdims=True)
-                    message[row + 1 : row + 2, p] = blank
-                edge = jnp.where(odd, first, last) if begin == 0 else jnp.where(odd, last, first)
-                message[row + 2 : row + 3, p] = edge
-                message[row + 3 : row + 4, p] = blank
+                row = 3 * k
+                for which in range(2) if k < 3 else (2,):
+                    weight = chosen[:, begin + which : begin + which + 1]
+                    put(message, row, i, jnp.sum(value * weight, axis=0, keepdims=True))
+                    row += 1
+                put(message, row, i, jnp.where(odd, first, last) if begin == 0 else jnp.where(odd, last, first))
 
 
 def slab_kernel(inner, after_one, after_two, sums):
@@ -203,29 +239,6 @@
         total += inner[peer]
     for peer in range(sums.shape[0]):
         sums[peer] = total
-
-
-def running_kernel(after, source, metric, lower, running, spread, held, held_metric, sems):
-    del after
-    pieces = pieces_of(source.shape[1])
-    metric_copy = pltpu.make_async_copy(metric, held_metric, sems.at[len(pieces)])
-    metric_copy.start()
-    copies = [pltpu.make_async_copy(source.at[:, p], held.at[:, p], sems.at[i]) for i, p in enumerate(pieces)]
-    for copy in copies:
-        copy.start()
-    metric_copy.wait()
-    stretch = column(held_metric[...])
-    spread[...] = jnp.broadcast_to(stretch, spread.shape)
-    scale = 1.0 / stretch
-    for i, p in enumerate(pieces):
-        copies[i].wait()
-        scaled = held[:, p] * scale
-        high = scaled.astype(jnp.bfloat16)
-        rest = scaled - high.astype(jnp.float32)
-        middle = rest.astype(jnp.bfloat16)
-        low = (rest - middle.astype(jnp.float32)).astype(jnp.bfloat16)
-        stacked = jnp.concatenate([high, middle, low], axis=0)
-        running[:, p] = jnp.dot(lower[...], stacked, preferred_element_type=jnp.float32)
 
 
 def velocity_kernel(place, slab, running, spread, inner, outer, velocity, offset, rate):
@@ -248,19 +261,18 @@
     rate[...] = jnp.broadcast_to(peak, rate.shape)
 
 
-def tendency_kernel(
-    kind, fields, source, velocity, offset, spread, message_one, message_two, curvature, table,
-    tendency, velocity_out,
-    held_fields, held_source, held_table, held_curvature, mixed, mixed_scalar, drift, sems,
+def inner_kernel(
+    kind, fields, source, velocity, spread, curvature, table,
+    partial, held_fields, edge_mixed, edge_scalar, edge_drift, velocity_out,
+    held_source, held_table, held_curvature, mixed, mixed_scalar, drift, sems,
 ):
     cells, lines = source.shape
-    pieces = pieces_of(lines)
     table_copy = pltpu.make_async_copy(table.at[kind[0]], held_table, sems.at[2, 0])
     table_copy.start()
     curvature_copy = pltpu.make_async_copy(curvature, held_curvature, sems.at[2, 1])
     curvature_copy.start()
     copies = []
-    for i, p in enumerate(pieces):
+    for i, p in enumerate(pieces_of(lines, STEPS // 2)):
         group = (
             pltpu.make_async_copy(source.at[:, p], held_source.at[:, p], sems.at[0, i]),
             pltpu.make_async_copy(fields.at[:, :, p], held_fields.at[:, :, p], sems.at[1, i]),
@@ -281,66 +293,90 @@
 
     def split(value):
         high, low = halves(value)
-        return jnp.where(is_low, low.astype(jnp.float32), high.astype(jnp.float32)).astype(jnp.bfloat16)
-
-    field_x = stretch * slope
+        return jnp.where(is_low, low.astype(jnp.float32), high.astype(jnp.float32))
+
+    field_x = split(stretch * slope)
     field_xx = stretch * stretch * bend + curving * slope
-    mixed[:cells, :] = split(field_x)
-    mixed[cells:, :] = split(VISCOSITY * field_xx)
-    mixed_scalar[:cells, :] = mixed[:cells, :]
-    mixed_scalar[cells:, :] = split(DIFFUSIVITY * field_xx)
-    drift[...] = split(stretch * held_table[2])
-
-    def stacked(value, tail):
+    tables_of = (
+        (mixed, edge_mixed, (field_x, split(VISCOSITY * field_xx))),
+        (mixed_scalar, edge_scalar, (field_x, split(DIFFUSIVITY * field_xx))),
+        (drift, edge_drift, (split(stretch * held_table[2]),)),
+    )
+    for whole, edge, values in tables_of:
+        for n, value in enumerate(values):
+            whole[n * cells : (n + 1) * cells, :] = value.astype(jnp.bfloat16)
+            edge[n * cells : (n + 1) * cells, :] = value[:, 3 * cells :].astype(jnp.bfloat16)
+
+    def stacked(value):
         high, low = halves(value)
-        tail_high = tail.astype(jnp.bfloat16).astype(jnp.float32)
-        tail_low = tail - tail_high
-        tails = jnp.concatenate(
-            [tail_high, tail_low, tail_high, jnp.zeros((DEPTH - 3 * cells - 24, CHUNK), jnp.float32)], axis=0
-        ).astype(jnp.bfloat16)
-        return jnp.concatenate([high, low, high, tails], axis=0)
-
-    for i, p in enumerate(pieces):
-        copies[i][0].wait()
+        return jnp.concatenate([high, low, high], axis=0)
+
+    depth = 3 * cells
+    for i, p in enumerate(pieces_of(lines)):
+        if i % 2 == 0:
+            copies[i // 2][0].wait()
         scaled = held_source[:, p] * (1.0 / stretch)
-        lead = message_one[12:16, p]
-        row = lax.broadcasted_iota(jnp.int32, lead.shape, 0)
-        lead = jnp.where(row == 1, offset[:, p], lead)
-        tail = jnp.concatenate([lead, message_two[12:16, p]], axis=0)
-        velocity_x = jnp.dot(drift[...], stacked(scaled, tail), preferred_element_type=jnp.float32)
+        velocity_x = jnp.dot(drift[:, :depth], stacked(scaled), preferred_element_type=jnp.float32)
         speed = velocity[:, p]
-        copies[i][1].wait()
+        if i % 2 == 0:
+            copies[i // 2][1].wait()
         for k in range(3):
             field = held_fields[k, :, p]
-            tail = jnp.concatenate([message_one[4 * k : 4 * k + 4, p], message_two[4 * k : 4 * k + 4, p]], axis=0)
             weights = mixed if k < 2 else mixed_scalar
-            both = jnp.dot(weights[...], stacked(field, tail), preferred_element_type=jnp.float32)
-            tendency[k, :, p] = both[cells:] - (speed * both[:cells] + field * velocity_x)
+            both = jnp.dot(weights[:, :depth], stacked(field), preferred_element_type=jnp.float32)
+            partial[k, :, p] = both[cells:] - (speed * both[:cells] + field * velocity_x)
     out_copy.wait()
 
 
+def tendency_kernel(
+    partial, fields, velocity, offset, edge_mixed, edge_scalar, edge_drift, message_one, message_two, tendency
+):
+    cells, lines = velocity.shape
+    width = lines // STEPS
+    blank = jnp.zeros((1, width), jnp.float32)
+    zeros = jnp.zeros((edge_mixed.shape[1] - 24, width), jnp.float32)
+
+    def tails(rows, part, second):
+        found = [[blank if row is None else take(message, row, part, width) for row in rows] for message in (message_one, message_two)]
+        tail = jnp.concatenate([found[0][0], found[0][1] if second is None else second, *found[0][2:], *found[1]], axis=0)
+        high = tail.astype(jnp.bfloat16).astype(jnp.float32)
+        return jnp.concatenate([high, tail - high, high, zeros], axis=0).astype(jnp.bfloat16)
+
+    for i, p in enumerate(pieces_of(lines)):
+        tail = tails((9, None, 10, None), i, offset[:, p])
+        velocity_x = jnp.dot(edge_drift[...], tail, preferred_element_type=jnp.float32)
+        speed = velocity[:, p]
+        for k in range(3):
+            tail = tails((3 * k, 3 * k + 1, 3 * k + 2, None), i, None)
+            weights = edge_mixed if k < 2 else edge_scalar
+            both = jnp.dot(weights[...], tail, preferred_element_type=jnp.float32)
+            tendency[k, :, p] = partial[k, :, p] + (both[cells:] - (speed * both[:cells] + fields[k, :, p] * velocity_x))
+
+
 def update_kernel(fields, register, tendency, rates, new_fields, new_register, held_fields, held_register, sems):
-    pieces = [(k, p) for k in range(3) for p in pieces_of(tendency.shape[2])]
+    cells = tendency.shape[1]
+    edges = [0, 3 * cells // 8, 3 * cells // 4, cells]
+    pieces = [(slice(None), slice(low, high)) for low, high in zip(edges[:-1], edges[1:])]
     arrivals = []
-    for i, (k, p) in enumerate(pieces):
+    for i, p in enumerate(pieces):
         pair = (
-            pltpu.make_async_copy(register.at[k, :, p], held_register.at[k, :, p], sems.at[0, i]),
-            pltpu.make_async_copy(fields.at[k, :, p], held_fields.at[k, :, p], sems.at[1, i]),
+            pltpu.make_async_copy(register.at[p], held_register.at[p], sems.at[0, i]),
+            pltpu.make_async_copy(fields.at[p], held_fields.at[p], sems.at[1, i]),
         )
         for copy in pair:
             copy.start()
         arrivals.append(pair)
     time_step = COURANT / jnp.max(jnp.max(rates[...], axis=0, keepdims=True), axis=1, keepdims=True)
     departures = []
-    for i, (k, p) in enumerate(pieces):
+    for i, p in enumerate(pieces):
         arrivals[i][0].wait()
-        updated = KEEP_FACTOR * held_register[k, :, p] + time_step * tendency[k, :, p]
-        held_register[k, :, p] = updated
-        departures.append(pltpu.make_async_copy(held_register.at[k, :, p], new_register.at[k, :, p], sems.at[2, i]))
+        updated = KEEP_FACTOR * held_register[p] + time_step * tendency[p]
+        held_register[p] = updated
+        departures.append(pltpu.make_async_copy(held_register.at[p], new_register.at[p], sems.at[2, i]))
         departures[-1].start()
         arrivals[i][1].wait()
-        held_fields[k, :, p] = held_fields[k, :, p] + STEP_FACTOR * updated
-        departures.append(pltpu.make_async_copy(held_fields.at[k, :, p], new_fields.at[k, :, p], sems.at[3, i]))
+        held_fields[p] = held_fields[p] + STEP_FACTOR * updated
+        departures.append(pltpu.make_async_copy(held_fields.at[p], new_fields.at[p], sems.at[3, i]))
         departures[-1].start()
     for copy in departures:
         copy.wait()
@@ -348,7 +384,6 @@
 
 def local(fields, register, source, metric, curvature):
     cells, lines = source.shape
-    steps = lines // CHUNK
     groups = lines // LANES
     inner_count, slab_count = lax.axis_size("inner"), lax.axis_size("slab")
     count = inner_count * slab_count
@@ -391,23 +426,32 @@
         in_specs=[hbm, hbm],
         out_specs=vmem,
         out_shape=fast(inner_count, groups, LANES),
-        scratch_shapes=[fast(cells, lines), one_row, semaphores((steps + 1,))],
+        scratch_shapes=[fast(cells, lines), one_row, semaphores((3,))],
         compiler_params=params,
         cost_estimate=cost(line_bytes),
         name="totals",
     )(source, metric_row)
     inner_totals = lax.all_to_all(totals, "inner", 0, 0)
 
-    message_one, message_two = pl.pallas_call(
+    lower = np.tril(np.ones((cells, cells))) - 0.5 * np.eye(cells)
+    lower = jnp.asarray(np.concatenate([lower] * 3, axis=1), jnp.bfloat16)
+    message_one, message_two, running, spread = pl.pallas_call(
         send_kernel,
-        in_specs=[smem, hbm, hbm, hbm, hbm],
-        out_specs=[vmem, vmem],
-        out_shape=[fast(MESSAGE, lines), fast(MESSAGE, lines)],
-        scratch_shapes=[fast(3, cells, lines), fast(cells, lines), one_row, fast(cells, LANES), semaphores((3, max(steps, 2)))],
+        in_specs=[smem, hbm, hbm, hbm, hbm, hbm],
+        out_specs=[vmem, vmem, vmem, vmem],
+        out_shape=[fast(*message_shape(lines)), fast(*message_shape(lines)), fast(cells, lines), fast(cells, LANES)],
+        scratch_shapes=[
+            fast(3, cells, lines),
+            fast(cells, lines),
+            one_row,
+            fast(cells, LANES),
+            pltpu.VMEM((cells, 3 * cells), jnp.bfloat16),
+            semaphores((3, 3)),
+        ],
         compiler_params=params,
         cost_estimate=cost(4 * line_bytes),
         name="send",
-    )(kind, fields, source, metric_row, far(jnp.asarray(send_weights)))
+    )(kind, fields, source, metric_row, far(jnp.asarray(send_weights)), far(lower))
 
     slab_sums = pl.pallas_call(
         slab_kernel,
@@ -422,21 +466,8 @@
     line = ("slab", "inner")
     even_pairs = [(i, i ^ 1) for i in range(count)]
     odd_pairs = [(i, i + 1 if i % 2 else i - 1) for i in range(1, count - 1)]
+    got_two = lax.ppermute(message_two, line, odd_pairs)
     got_one = lax.ppermute(message_one, line, even_pairs)
-    got_two = lax.ppermute(message_two, line, odd_pairs)
-
-    lower = np.tril(np.ones((cells, cells))) - 0.5 * np.eye(cells)
-    lower = jnp.asarray(np.concatenate([lower] * 3, axis=1), jnp.bfloat16)
-    running, spread = pl.pallas_call(
-        running_kernel,
-        in_specs=[hbm, hbm, hbm, vmem],
-        out_specs=[vmem, vmem],
-        out_shape=[fast(cells, lines), fast(cells, LANES)],
-        scratch_shapes=[fast(cells, lines), one_row, semaphores((steps + 1,))],
-        compiler_params=params,
-        cost_estimate=cost(2 * line_bytes),
-        name="running",
-    )(slab_sums, source, metric_row, lower)
 
     velocity, offset, rate = pl.pallas_call(
         velocity_kernel,
@@ -450,27 +481,47 @@
 
     rates = lax.all_to_all(rate, ("slab", "inner", "gz"), 0, 0, tiled=True)
 
-    tendency, velocity_out = pl.pallas_call(
-        tendency_kernel,
-        in_specs=[smem, hbm, hbm, vmem, vmem, vmem, vmem, vmem, hbm, hbm],
-        out_specs=[vmem, hbm],
-        out_shape=[fast(3, cells, lines), pltpu.HBM((cells, lines), jnp.float32)],
+    def half(*sizes):
+        return pltpu.VMEM(sizes, jnp.bfloat16)
+
+    edge = DEPTH - 3 * cells
+    partial, held_fields, edge_mixed, edge_scalar, edge_drift, velocity_out = pl.pallas_call(
+        inner_kernel,
+        in_specs=[smem, hbm, hbm, vmem, vmem, hbm, hbm],
+        out_specs=[vmem, vmem, vmem, vmem, vmem, hbm],
+        out_shape=[
+            fast(3, cells, lines),
+            fast(3, cells, lines),
+            half(2 * cells, edge),
+            half(2 * cells, edge),
+            half(cells, edge),
+            pltpu.HBM((cells, lines), jnp.float32),
+        ],
         scratch_shapes=[
-            fast(3, cells, lines),
             fast(cells, lines),
             fast(3, cells, DEPTH),
             one_row,
-            pltpu.VMEM((2 * cells, DEPTH), jnp.bfloat16),
-            pltpu.VMEM((2 * cells, DEPTH), jnp.bfloat16),
-            pltpu.VMEM((cells, DEPTH), jnp.bfloat16),
-            semaphores((3, max(steps, 3))),
+            half(2 * cells, DEPTH),
+            half(2 * cells, DEPTH),
+            half(cells, DEPTH),
+            semaphores((3, 3)),
         ],
         compiler_params=params,
         cost_estimate=cost(12 * line_bytes),
+        name="inner",
+    )(kind, fields, source, keep(velocity), keep(spread), curvature_row, far(jnp.asarray(solve_tables)))
+
+    tendency = pl.pallas_call(
+        tendency_kernel,
+        in_specs=[vmem] * 9,
+        out_specs=vmem,
+        out_shape=fast(3, cells, lines),
+        compiler_params=params,
+        cost_estimate=cost(8 * line_bytes),
         name="tendency",
     )(
-        kind, fields, source, keep(velocity), keep(offset), keep(spread), got_one, got_two, curvature_row,
-        far(jnp.asarray(solve_tables)),
+        keep(partial), keep(held_fields), keep(velocity), keep(offset), keep(edge_mixed), keep(edge_scalar),
+        keep(edge_drift), got_one, got_two,
     )
 
     new_fields, new_register = pl.pallas_call(
@@ -478,7 +529,7 @@
         in_specs=[hbm, hbm, vmem, vmem],
         out_specs=[hbm, hbm],
         out_shape=[pltpu.HBM((3, cells, lines), jnp.float32)] * 2,
-        scratch_shapes=[fast(3, cells, lines), fast(3, cells, lines), semaphores((4, 3 * steps))],
+        scratch_shapes=[fast(3, cells, lines), fast(3, cells, lines), semaphores((4, 3))],
         compiler_params=params,
         cost_estimate=cost(12 * line_bytes),
         name="update",

time: 56.6 us -> 54.3 us (0.959)
  blocking collectives: 0 us -> 14.9 us
  waiting for transfers between devices: 14 us -> 5.94 us
  starting transfers between devices: 25.9 us -> 18.5 us
  Pallas kernels: 15.5 us -> 14 us
    all_to_all x0 -> x1, blocking collectives: none -> 14.9 us  [local(): slab_totals = lax.all_to_all(slab_sums, 'slab', 0, 0)]
    all_to_all x1 -> x0, starting transfers between devices: 7.46 us -> none  [local(): slab_totals = lax.all_to_all(slab_sums, 'slab', 0, 0)]
    all_to_all x1 -> x0, waiting for transfers between devices: 6.06 us -> none  [local(): slab_totals = lax.all_to_all(slab_sums, 'slab', 0, 0)]
    ppermute x1, waiting for transfers between devices: 5.59 us -> 1.5 us  [local(): got_two = lax.ppermute(message_two, line, odd_pairs)]
    all_to_all x1, waiting for transfers between devices: 0.01 us -> 2.57 us  [local(): rates = lax.all_to_all(rate, ('slab', 'inner', 'gz'), 0, 0, tiled=True)]
    pallas_call x1, Pallas kernels: 4.42 us -> 3.59 us  [local(): pl.pallas_call(update_kernel, in_specs=[hbm, hbm, vmem, vmem], out_specs=...]
    pallas_call x1, Pallas kernels: 0.65 us -> 0.01 us  [local(): pl.pallas_call(slab_kernel, in_specs=[vmem, hbm, hbm], out_specs=vmem, ou...]
  transfers between devices with their start and end apart: 5 -> 4, of which waited for: 3 -> 3; matrix products, arithmetic and copies ran while one was open for 0% -> 0% of each run, Pallas kernels for 9% -> 8%
where the time goes in v3:
time: 54.3 us; the launch traced here: 54 us
  starting transfers between devices  18.5 us (34%)
  blocking collectives  14.9 us (27%)
  Pallas kernels  14 us (26%)
  waiting for transfers between devices  5.94 us (11%)
  between operations  0.69 us (1%)
    all_to_all x1, blocking collectives, local(): slab_totals = lax.all_to_all(slab_sums, 'slab', 0, 0)  14.9 us
    all_to_all x1, starting transfers between devices, local(): rates = lax.all_to_all(rate, ('slab', 'inner', 'gz'), 0, 0, tiled=True)  7.82 us
    all_to_all x1, starting transfers between devices, local(): inner_totals = lax.all_to_all(totals, 'inner', 0, 0)  6.52 us
    pallas_call x1, Pallas kernels, local(): pl.pallas_call(update_kernel, in_specs=[hbm, hbm, vmem, vmem], out_specs=...  3.59 us
    pallas_call x1, Pallas kernels, local(): pl.pallas_call(inner_kernel, in_specs=[smem, hbm, hbm, vmem, vmem, hbm, h...  3.4 us
    pallas_call x1, Pallas kernels, local(): pl.pallas_call(send_kernel, in_specs=[smem, hbm, hbm, hbm, hbm, hbm], out...  3.13 us
    all_to_all x1, waiting for transfers between devices, local(): rates = lax.all_to_all(rate, ('slab', 'inner', 'gz'), 0, 0, tiled=True)  2.57 us
    ppermute x1, starting transfers between devices, local(): got_one = lax.ppermute(message_one, line, even_pairs)  2.23 us
  transfers between devices with their start and end apart: 4, of which 3 were waited for; matrix products, arithmetic and copies ran while one was open for 0% of the time, Pallas kernels for 8%

profile of v3, /device:TPU:1, one launch (start us, length us, event | category | flops | bytes accessed | tf_op | source)
XLA Modules:
  0.0 54.0 jit_solution(12552343687425329358)
XLA Ops:
  0.6 1.9 %totals.1 = f32[8,24,128]{2,1,0:T(8,128)} custom-call(f32[64,3072]{1,0:T(8,128)} %source.5, f32[1,64]{1,0:T(1,128)} %bitcast.10), custom_call_target="tpu_custom_call" | custom-call | bytes 786432 | tf_op jit(solution)/shard_map/totals/pallas_call | solution.py:424
  2.5 6.5 %all-to-all-start = ((f32[8,24,128]{2,1,0:T(8,128)}), f32[8,24,128]{2,1,0:T(8,128)S(1)}, u32[]{:S(2)}, u32[]{:S(2)}) async-start(f32[8,24,128]{2,1,0:T(8,128)} %totals.1), calls=%async_computation | async-start | bytes 196608 | tf_op jit(solution)/shard_map/all_to_all | solution.py:434
  9.0 3.1 %send.1 = (f32[8,4224]{1,0:T(8,128)S(1)}, f32[8,4224]{1,0:T(8,128)S(1)}, f32[64,3072]{1,0:T(8,128)S(1)}, f32[64,128]{1,0:T(8,128)S(1)}) custom-call(s32[1]{0:T(128)} %bitcast.kind, f32[3,64,3072]{2,1,0:T(8,128)} %fields.5, f32[64,3072]{1,0:T(8,128)} %source.5, f32[1,64]{1,0:T(1,128)} %bitcast.11, f32[4,64,128]{2,1,0:T(8,128)} %constant.38.clone.weights, ...), custom_call_target="tpu_custom_call" | custom-call | bytes 3145728 | tf_op jit(solution)/shard_map/send/pallas_call | solution.py:438
  12.1 1.9 %all-to-all-done.inner = f32[8,24,128]{2,1,0:T(8,128)S(1)} async-done(((f32[8,24,128]{2,1,0:T(8,128)}), f32[8,24,128]{2,1,0:T(8,128)S(1)}, u32[]{:S(2)}, u32[]{:S(2)}) %all-to-all-start) | async-done | bytes 98336 | tf_op jit(solution)/shard_map/all_to_all | solution.py:434
  14.0 14.9 %all_to_all.21.outer = f32[8,24,128]{2,1,0:T(8,128)S(1)} all-to-all(f32[8,24,128]{2,1,0:T(8,128)S(1)} %slab.1), channel_id=1, replica_groups=mesh['slab'=8,'inner'=8,'gz'=4] {'slab'}, dimensions={0} | all-to-all | bytes 196608 | tf_op jit(solution)/shard_map/all_to_all | solution.py:464
  29.0 1.0 %velocity.1 = (f32[64,3072]{1,0:T(8,128)S(1)}, f32[1,3072]{1,0:T(1,128)S(1)}, f32[256,128]{1,0:T(8,128)}) custom-call(s32[1]{0:T(128)} %bitcast.1.place, s32[1]{0:T(128)} %bitcast.2.slab, f32[64,3072]{1,0:T(8,128)S(1)} %get-tuple-element.18.running, f32[64,128]{1,0:T(8,128)S(1)} %get-tuple-element.19.spread, f32[8,24,128]{2,1,0:T(8,128)S(1)} %all-to-all-done.inner, ...), custom_call_target="tpu_custom_call" | custom-call | bytes 1572864 | tf_op jit(solution)/shard_map/velocity/pallas_call | solution.py:472
  29.9 7.8 %all-to-all-start.2 = ((f32[256,1,128]{2,1,0:T(1,128)}), f32[256,1,128]{2,1,0:T(1,128)S(1)}, u32[]{:S(2)}, u32[]{:S(2)}) async-start(f32[256,1,128]{2,1,0:T(1,128)} %bitcast.6), calls=%async_computation.2 | async-start | bytes 262144 | tf_op jit(solution)/shard_map/all_to_all | solution.py:482
  37.8 2.2 %collective-permute-start = (f32[8,4224]{1,0:T(8,128)S(1)}, f32[8,4224]{1,0:T(8,128)S(1)}, u32[]{:S(2)}, u32[]{:S(2)}) collective-permute-start(f32[8,4224]{1,0:T(8,128)S(1)} %get-tuple-element.20.after_one), channel_id=1, source_target_pairs={{0,4},{4,0},{8,12},{12,8},{16,20},{20,16},{24,28},{28,24},{32,36},... | collective-permute-start | bytes 405512 | tf_op jit(solution)/shard_map/ppermute | solution.py:470
  40.0 1.9 %collective-permute-start.1 = (f32[8,4224]{1,0:T(8,128)S(1)}, f32[8,4224]{1,0:T(8,128)S(1)}, u32[]{:S(2)}, u32[]{:S(2)}) collective-permute-start(f32[8,4224]{1,0:T(8,128)S(1)} %get-tuple-element.21.after_two), channel_id=1, source_target_pairs={{4,8},{8,4},{12,16},{16,12},{20,24},{24,20},{28,32},{32,28},{36,40... | collective-permute-start | bytes 405512 | tf_op jit(solution)/shard_map/ppermute | solution.py:469
  41.9 3.4 %inner.1 = (f32[3,64,3072]{2,1,0:T(8,128)S(1)}, f32[3,64,3072]{2,1,0:T(8,128)S(1)}, bf16[128,64]{1,0:T(8,128)(2,1)S(1)}, bf16[128,64]{1,0:T(8,128)(2,1)S(1)}, bf...) custom-call(s32[1]{0:T(128)} %bitcast.kind, f32[3,64,3072]{2,1,0:T(8,128)} %fields.5, f32[64,3072]{1,0:T(8,128)} %source.5, ...), custom_call_target="tpu_custom_call" | custom-call | bytes 9437184 | tf_op jit(solution)/shard_map/inner/pallas_call | solution.py:488
  45.3 0.0 collective-permute-done.message_one
  45.3 1.5 %collective-permute-done.1.message_two = f32[8,4224]{1,0:T(8,128)S(1)} collective-permute-done((f32[8,4224]{1,0:T(8,128)S(1)}, f32[8,4224]{1,0:T(8,128)S(1)}, u32[]{:S(2)}, u32[]{:S(2)}) %collective-permute-start.1) | collective-permute-done | bytes 135200 | tf_op jit(solution)/shard_map/ppermute | solution.py:469
  46.8 1.0 %tendency.1 = f32[3,64,3072]{2,1,0:T(8,128)S(1)} custom-call(f32[3,64,3072]{2,1,0:T(8,128)S(1)} %get-tuple-element.23.partial, f32[3,64,3072]{2,1,0:T(8,128)S(1)} %get-tuple-element.24.fields, f32[64,3072]{1,0:T(8,128)S(1)} %get-tuple-element.22.velocity, f32[1,3072]{1,0:T(1,128)S(1)} %get-tuple-element.25.offset, ...), custom_call_target="tpu_custom_call" | custom-call | bytes 6291456 | tf_op jit(solution)/shard_map/tendency/pallas_call | solution.py:514
  47.8 2.6 %all-to-all-done.2 = f32[256,1,128]{2,1,0:T(1,128)S(1)} async-done(((f32[256,1,128]{2,1,0:T(1,128)}), f32[256,1,128]{2,1,0:T(1,128)S(1)}, u32[]{:S(2)}, u32[]{:S(2)}) %all-to-all-start.2) | async-done | bytes 131104 | tf_op jit(solution)/shard_map/all_to_all | solution.py:482
  50.4 3.6 %update.1 = (f32[3,64,3072]{2,1,0:T(8,128)}, f32[3,64,3072]{2,1,0:T(8,128)}) custom-call(f32[3,64,3072]{2,1,0:T(8,128)} %fields.5, f32[3,64,3072]{2,1,0:T(8,128)} %register.1, f32[3,64,3072]{2,1,0:T(8,128)S(1)} %tendency.1, f32[256,128]{1,0:T(8,128)S(1)} %bitcast.9), custom_call_target="tpu_custom_call" | custom-call | bytes 9437184 | tf_op jit(solution)/shard_map/update/pallas_call | solution.py:527
  (1 shorter events, 0.0 us)
Async XLA Ops:
  2.5 11.5 %all-to-all-start = ((f32[8,24,128]{2,1,0:T(8,128)}), f32[8,24,128]{2,1,0:T(8,128)S(1)}, u32[]{:S(2)}, u32[]{:S(2)}) async-start(f32[8,24,128]{2,1,0:T(8,128)} %totals.1), calls=%async_computation | async-start | bytes 196608 | tf_op jit(solution)/shard_map/all_to_all | solution.py:434
  29.9 20.5 %all-to-all-start.2 = ((f32[256,1,128]{2,1,0:T(1,128)}), f32[256,1,128]{2,1,0:T(1,128)S(1)}, u32[]{:S(2)}, u32[]{:S(2)}) async-start(f32[256,1,128]{2,1,0:T(1,128)} %bitcast.6), calls=%async_computation.2 | async-start | bytes 262144 | tf_op jit(solution)/shard_map/all_to_all | solution.py:482
  37.8 7.6 %collective-permute-start = (f32[8,4224]{1,0:T(8,128)S(1)}, f32[8,4224]{1,0:T(8,128)S(1)}, u32[]{:S(2)}, u32[]{:S(2)}) collective-permute-start(f32[8,4224]{1,0:T(8,128)S(1)} %get-tuple-element.20.after_one), channel_id=1, source_target_pairs={{0,4},{4,0},{8,12},{12,8},{16,20},{20,16},{24,28},{28,24},{32,36},... | collective-permute-start | bytes 405512 | tf_op jit(solution)/shard_map/ppermute | solution.py:470
  40.0 6.8 %collective-permute-start.1 = (f32[8,4224]{1,0:T(8,128)S(1)}, f32[8,4224]{1,0:T(8,128)S(1)}, u32[]{:S(2)}, u32[]{:S(2)}) collective-permute-start(f32[8,4224]{1,0:T(8,128)S(1)} %get-tuple-element.21.after_two), channel_id=1, source_target_pairs={{4,8},{8,4},{12,16},{16,12},{20,24},{24,20},{28,32},{32,28},{36,40... | collective-permute-start | bytes 405512 | tf_op jit(solution)/shard_map/ppermute | solution.py:469

commit v4 on v3

--- a/solution.py
+++ b/solution.py
@@ -22,6 +22,9 @@
 STEP_FACTOR = 15.0 / 16.0
 
 LANES = 128
+SLAB_FIRST = 4
+INNER_FIRST = 0
+RATE_FIRST = (4, 2, 2)
 STEPS = 4
 GRANT = 24 * 1024 * 1024
 MESSAGE = 11
@@ -246,9 +249,11 @@
     squared = 4.0 * VISCOSITY * stretch * stretch
     before = jnp.zeros(inner.shape[1:], jnp.float32)
     for peer in range(inner.shape[0]):
-        before += jnp.where(peer < place[0], inner[peer], 0.0)
+        owner = (peer + INNER_FIRST) % inner.shape[0]
+        before += jnp.where(owner < place[0], inner[peer], 0.0)
     for peer in range(outer.shape[0]):
-        before += jnp.where(peer < slab[0], outer[peer], 0.0)
+        owner = (peer + SLAB_FIRST) % outer.shape[0]
+        before += jnp.where(owner < slab[0], outer[peer], 0.0)
     top = jnp.zeros((1, LANES), jnp.float32)
     for k in range(before.shape[0]):
         here = slice(k * LANES, (k + 1) * LANES)
@@ -261,18 +266,19 @@
     rate[...] = jnp.broadcast_to(peak, rate.shape)
 
 
-def inner_kernel(
-    kind, fields, source, velocity, spread, curvature, table,
-    partial, held_fields, edge_mixed, edge_scalar, edge_drift, velocity_out,
-    held_source, held_table, held_curvature, mixed, mixed_scalar, drift, sems,
+def tendency_kernel(
+    kind, fields, source, velocity, offset, spread, message_one, message_two, curvature, table,
+    tendency, velocity_out,
+    held_fields, held_source, held_table, held_curvature, mixed, mixed_scalar, drift, sems,
 ):
     cells, lines = source.shape
+    pieces = pieces_of(lines, STEPS // 2)
     table_copy = pltpu.make_async_copy(table.at[kind[0]], held_table, sems.at[2, 0])
     table_copy.start()
     curvature_copy = pltpu.make_async_copy(curvature, held_curvature, sems.at[2, 1])
     curvature_copy.start()
     copies = []
-    for i, p in enumerate(pieces_of(lines, STEPS // 2)):
+    for i, p in enumerate(pieces):
         group = (
             pltpu.make_async_copy(source.at[:, p], held_source.at[:, p], sems.at[0, i]),
             pltpu.make_async_copy(fields.at[:, :, p], held_fields.at[:, :, p], sems.at[1, i]),
@@ -293,67 +299,51 @@
 
     def split(value):
         high, low = halves(value)
-        return jnp.where(is_low, low.astype(jnp.float32), high.astype(jnp.float32))
-
-    field_x = split(stretch * slope)
+        return jnp.where(is_low, low.astype(jnp.float32), high.astype(jnp.float32)).astype(jnp.bfloat16)
+
+    field_x = stretch * slope
     field_xx = stretch * stretch * bend + curving * slope
-    tables_of = (
-        (mixed, edge_mixed, (field_x, split(VISCOSITY * field_xx))),
-        (mixed_scalar, edge_scalar, (field_x, split(DIFFUSIVITY * field_xx))),
-        (drift, edge_drift, (split(stretch * held_table[2]),)),
-    )
-    for whole, edge, values in tables_of:
-        for n, value in enumerate(values):
-            whole[n * cells : (n + 1) * cells, :] = value.astype(jnp.bfloat16)
-            edge[n * cells : (n + 1) * cells, :] = value[:, 3 * cells :].astype(jnp.bfloat16)
-
-    def stacked(value):
+    mixed[:cells, :] = split(field_x)
+    mixed[cells:, :] = split(VISCOSITY * field_xx)
+    mixed_scalar[:cells, :] = mixed[:cells, :]
+    mixed_scalar[cells:, :] = split(DIFFUSIVITY * field_xx)
+    drift[...] = split(stretch * held_table[2])
+
+    def stacked(value, tail):
         high, low = halves(value)
-        return jnp.concatenate([high, low, high], axis=0)
-
-    depth = 3 * cells
+        tail_high = tail.astype(jnp.bfloat16).astype(jnp.float32)
+        tail_low = tail - tail_high
+        tails = jnp.concatenate(
+            [tail_high, tail_low, tail_high, jnp.zeros((DEPTH - 3 * cells - 24, width), jnp.float32)], axis=0
+        ).astype(jnp.bfloat16)
+        return jnp.concatenate([high, low, high, tails], axis=0)
+
+    width = lines // STEPS
+    blank = jnp.zeros((1, width), jnp.float32)
+
+    def tails(rows, part, second):
+        found = [[blank if row is None else take(message, row, part, width) for row in rows] for message in (message_one, message_two)]
+        return jnp.concatenate([found[0][0], found[0][1] if second is None else second, *found[0][2:], *found[1]], axis=0)
+
     for i, p in enumerate(pieces_of(lines)):
         if i % 2 == 0:
             copies[i // 2][0].wait()
         scaled = held_source[:, p] * (1.0 / stretch)
-        velocity_x = jnp.dot(drift[:, :depth], stacked(scaled), preferred_element_type=jnp.float32)
+        tail = tails((9, None, 10, None), i, offset[:, p])
+        velocity_x = jnp.dot(drift[...], stacked(scaled, tail), preferred_element_type=jnp.float32)
         speed = velocity[:, p]
         if i % 2 == 0:
             copies[i // 2][1].wait()
         for k in range(3):
             field = held_fields[k, :, p]
+            tail = tails((3 * k, 3 * k + 1, 3 * k + 2, None), i, None)
             weights = mixed if k < 2 else mixed_scalar
-            both = jnp.dot(weights[:, :depth], stacked(field), preferred_element_type=jnp.float32)
-            partial[k, :, p] = both[cells:] - (speed * both[:cells] + field * velocity_x)
+            both = jnp.dot(weights[...], stacked(field, tail), preferred_element_type=jnp.float32)
+            tendency[k, :, p] = both[cells:] - (speed * both[:cells] + field * velocity_x)
     out_copy.wait()
 
 
-def tendency_kernel(
-    partial, fields, velocity, offset, edge_mixed, edge_scalar, edge_drift, message_one, message_two, tendency
-):
-    cells, lines = velocity.shape
-    width = lines // STEPS
-    blank = jnp.zeros((1, width), jnp.float32)
-    zeros = jnp.zeros((edge_mixed.shape[1] - 24, width), jnp.float32)
-
-    def tails(rows, part, second):
-        found = [[blank if row is None else take(message, row, part, width) for row in rows] for message in (message_one, message_two)]
-        tail = jnp.concatenate([found[0][0], found[0][1] if second is None else second, *found[0][2:], *found[1]], axis=0)
-        high = tail.astype(jnp.bfloat16).astype(jnp.float32)
-        return jnp.concatenate([high, tail - high, high, zeros], axis=0).astype(jnp.bfloat16)
-
-    for i, p in enumerate(pieces_of(lines)):
-        tail = tails((9, None, 10, None), i, offset[:, p])
-        velocity_x = jnp.dot(edge_drift[...], tail, preferred_element_type=jnp.float32)
-        speed = velocity[:, p]
-        for k in range(3):
-            tail = tails((3 * k, 3 * k + 1, 3 * k + 2, None), i, None)
-            weights = edge_mixed if k < 2 else edge_scalar
-            both = jnp.dot(weights[...], tail, preferred_element_type=jnp.float32)
-            tendency[k, :, p] = partial[k, :, p] + (both[cells:] - (speed * both[:cells] + fields[k, :, p] * velocity_x))
-
-
-def update_kernel(fields, register, tendency, rates, new_fields, new_register, held_fields, held_register, sems):
+def update_kernel(fields, register, tendency, rates, more_rates, new_fields, new_register, held_fields, held_register, sems):
     cells = tendency.shape[1]
     edges = [0, 3 * cells // 8, 3 * cells // 4, cells]
     pieces = [(slice(None), slice(low, high)) for low, high in zip(edges[:-1], edges[1:])]
@@ -366,7 +356,8 @@
         for copy in pair:
             copy.start()
         arrivals.append(pair)
-    time_step = COURANT / jnp.max(jnp.max(rates[...], axis=0, keepdims=True), axis=1, keepdims=True)
+    highest = jnp.maximum(rates[...], more_rates[...])
+    time_step = COURANT / jnp.max(jnp.max(highest, axis=0, keepdims=True), axis=1, keepdims=True)
     departures = []
     for i, p in enumerate(pieces):
         arrivals[i][0].wait()
@@ -382,13 +373,18 @@
         copy.wait()
 
 
+def turned(first, count):
+    return [[(i + first) % count for i in range(count)]]
+
+
 def local(fields, register, source, metric, curvature):
     cells, lines = source.shape
     groups = lines // LANES
-    inner_count, slab_count = lax.axis_size("inner"), lax.axis_size("slab")
+    near, line, same_core = ("ring", "core"), ("slab", "ring", "core"), ("slab", "ring", "gz")
+    inner_count, slab_count = lax.axis_size(near), lax.axis_size("slab")
     count = inner_count * slab_count
-    devices = count * lax.axis_size("gz")
-    inner, slab = lax.axis_index("inner"), lax.axis_index("slab")
+    devices = lax.axis_size(same_core)
+    inner, slab = lax.axis_index(near), lax.axis_index("slab")
     position = slab * inner_count + inner
     kind = jnp.where(position == 0, 0, jnp.where(position == count - 1, 3, 1 + position % 2))
     kind, inner, slab = (jnp.reshape(value, (1,)).astype(jnp.int32) for value in (kind, inner, slab))
@@ -431,7 +427,7 @@
         cost_estimate=cost(line_bytes),
         name="totals",
     )(source, metric_row)
-    inner_totals = lax.all_to_all(totals, "inner", 0, 0)
+    inner_totals = lax.all_to_all(totals, near, 0, 0, axis_index_groups=turned(INNER_FIRST, inner_count))
 
     lower = np.tril(np.ones((cells, cells))) - 0.5 * np.eye(cells)
     lower = jnp.asarray(np.concatenate([lower] * 3, axis=1), jnp.bfloat16)
@@ -461,9 +457,8 @@
         compiler_params=params,
         name="slab",
     )(keep(inner_totals), message_one, message_two)
-    slab_totals = lax.all_to_all(slab_sums, "slab", 0, 0)
-
-    line = ("slab", "inner")
+    slab_totals = lax.all_to_all(slab_sums, "slab", 0, 0, axis_index_groups=turned(SLAB_FIRST, slab_count))
+
     even_pairs = [(i, i ^ 1) for i in range(count)]
     odd_pairs = [(i, i + 1 if i % 2 else i - 1) for i in range(1, count - 1)]
     got_two = lax.ppermute(message_two, line, odd_pairs)
@@ -479,61 +474,45 @@
         name="velocity",
     )(inner, slab, keep(running), keep(spread), keep(inner_totals), keep(slab_totals))
 
-    rates = lax.all_to_all(rate, ("slab", "inner", "gz"), 0, 0, tiled=True)
-
-    def half(*sizes):
-        return pltpu.VMEM(sizes, jnp.bfloat16)
-
-    edge = DEPTH - 3 * cells
-    partial, held_fields, edge_mixed, edge_scalar, edge_drift, velocity_out = pl.pallas_call(
-        inner_kernel,
-        in_specs=[smem, hbm, hbm, vmem, vmem, hbm, hbm],
-        out_specs=[vmem, vmem, vmem, vmem, vmem, hbm],
-        out_shape=[
+    order = np.arange(devices).reshape([lax.axis_size(axis) for axis in same_core])
+    order = [int(i) for i in np.roll(order, [-turn for turn in RATE_FIRST], axis=(0, 1, 2)).ravel()]
+    rates = lax.all_to_all(rate, same_core, 0, 0, axis_index_groups=[order], tiled=True)
+
+    tendency, velocity_out = pl.pallas_call(
+        tendency_kernel,
+        in_specs=[smem, hbm, hbm, vmem, vmem, vmem, vmem, vmem, hbm, hbm],
+        out_specs=[vmem, hbm],
+        out_shape=[fast(3, cells, lines), pltpu.HBM((cells, lines), jnp.float32)],
+        scratch_shapes=[
             fast(3, cells, lines),
-            fast(3, cells, lines),
-            half(2 * cells, edge),
-            half(2 * cells, edge),
-            half(cells, edge),
-            pltpu.HBM((cells, lines), jnp.float32),
-        ],
-        scratch_shapes=[
             fast(cells, lines),
             fast(3, cells, DEPTH),
             one_row,
-            half(2 * cells, DEPTH),
-            half(2 * cells, DEPTH),
-            half(cells, DEPTH),
+            pltpu.VMEM((2 * cells, DEPTH), jnp.bfloat16),
+            pltpu.VMEM((2 * cells, DEPTH), jnp.bfloat16),
+            pltpu.VMEM((cells, DEPTH), jnp.bfloat16),
             semaphores((3, 3)),
         ],
         compiler_params=params,
         cost_estimate=cost(12 * line_bytes),
-        name="inner",
-    )(kind, fields, source, keep(velocity), keep(spread), curvature_row, far(jnp.asarray(solve_tables)))
-
-    tendency = pl.pallas_call(
-        tendency_kernel,
-        in_specs=[vmem] * 9,
-        out_specs=vmem,
-        out_shape=fast(3, cells, lines),
-        compiler_params=params,
-        cost_estimate=cost(8 * line_bytes),
         name="tendency",
     )(
-        keep(partial), keep(held_fields), keep(velocity), keep(offset), keep(edge_mixed), keep(edge_scalar),
-        keep(edge_drift), got_one, got_two,
+        kind, fields, source, keep(velocity), keep(offset), keep(spread), got_one, got_two, curvature_row,
+        far(jnp.asarray(solve_tables)),
     )
 
+    rates, tendency = lax.optimization_barrier((rates, tendency))
+    more_rates = lax.ppermute(rates, "core", [(0, 1), (1, 0)])
     new_fields, new_register = pl.pallas_call(
         update_kernel,
-        in_specs=[hbm, hbm, vmem, vmem],
+        in_specs=[hbm, hbm, vmem, vmem, vmem],
         out_specs=[hbm, hbm],
         out_shape=[pltpu.HBM((3, cells, lines), jnp.float32)] * 2,
         scratch_shapes=[fast(3, cells, lines), fast(3, cells, lines), semaphores((4, 3))],
         compiler_params=params,
         cost_estimate=cost(12 * line_bytes),
         name="update",
-    )(fields, register, keep(tendency), rates)
+    )(fields, register, keep(tendency), keep(rates), keep(more_rates))
     return (new_fields, new_register, velocity_out)
 
 
@@ -542,8 +521,9 @@
     inner = 1
     while inner * inner < along:
         inner *= 2
-    split = Mesh(mesh.devices.reshape(along // inner, inner, across), ("slab", "inner", "gz"))
-    line = ("slab", "inner")
+    shape = (along // inner, inner // 2, 2, across)
+    split = Mesh(mesh.devices.reshape(shape), ("slab", "ring", "core", "gz"))
+    line = ("slab", "ring", "core")
     placed = (P(None, line, "gz"), P(None, line, "gz"), P(line, "gz"), P(line), P(line))
     return jax.shard_map(
         local,

time: 54.3 us -> 52.8 us (0.972)
  starting transfers between devices: 18.5 us -> 35.3 us
  blocking collectives: 14.9 us -> 0 us
  waiting for transfers between devices: 5.94 us -> 2.78 us
    all_to_all x2 -> x3, starting transfers between devices: 14.3 us -> 30.7 us  [the longest x1 14.7 us: local(): lax.all_to_all(rate, same_core, 0, 0, axis_index_groups=[order], tiled=True)]
    all_to_all x1 -> x0, blocking collectives: 14.9 us -> none  [local(): slab_totals = lax.all_to_all(slab_sums, 'slab', 0, 0)]
    all_to_all x2 -> x3, waiting for transfers between devices: 4.44 us -> 1.87 us  [the longest x1 1.87 us: local(): lax.all_to_all(totals, near, 0, 0, axis_index_groups=turned(INNER_FIRST,...]
    ppermute x1, waiting for transfers between devices: 1.5 us -> 0.01 us  [local(): got_two = lax.ppermute(message_two, line, odd_pairs)]
    ppermute x0 -> x1, starting transfers between devices: none -> 1.41 us  [local(): more_rates = lax.ppermute(rates, 'core', [(0, 1), (1, 0)])]
    ppermute x1, starting transfers between devices: 2.23 us -> 1.1 us  [local(): got_one = lax.ppermute(message_one, line, even_pairs)]
    pallas_call x3 -> x2, Pallas kernels: 8 us -> 7.03 us  [the longest x1 3.59 us: local(): pl.pallas_call(update_kernel, in_specs=[hbm, hbm, vmem, vmem, vmem], out_...]
    ppermute x0 -> x1, waiting for transfers between devices: none -> 0.9 us  [local(): more_rates = lax.ppermute(rates, 'core', [(0, 1), (1, 0)])]
  transfers between devices with their start and end apart: 4 -> 6, of which waited for: 3 -> 2; matrix products, arithmetic and copies ran while one was open for 0% -> 0% of each run, Pallas kernels for 8% -> 8%
where the time goes in v4:
time: 52.8 us; the launch traced here: 52.4 us
  starting transfers between devices  35.3 us (67%)
  Pallas kernels  13.6 us (26%)
  waiting for transfers between devices  2.78 us (5%)
  between operations  0.7 us (1%)
    all_to_all x1, starting transfers between devices, local(): lax.all_to_all(rate, same_core, 0, 0, axis_index_groups=[order], tiled=True)  14.7 us
    all_to_all x1, starting transfers between devices, local(): lax.all_to_all(slab_sums, 'slab', 0, 0, axis_index_groups=turned(SLAB_FIR...  9.47 us
    all_to_all x1, starting transfers between devices, local(): lax.all_to_all(totals, near, 0, 0, axis_index_groups=turned(INNER_FIRST,...  6.52 us
    pallas_call x1, Pallas kernels, local(): pl.pallas_call(update_kernel, in_specs=[hbm, hbm, vmem, vmem, vmem], out_...  3.59 us
    pallas_call x1, Pallas kernels, local(): pl.pallas_call(tendency_kernel, in_specs=[smem, hbm, hbm, vmem, vmem, vme...  3.44 us
    pallas_call x1, Pallas kernels, local(): pl.pallas_call(send_kernel, in_specs=[smem, hbm, hbm, hbm, hbm, hbm], out...  3.13 us
    ppermute x1, starting transfers between devices, local(): got_two = lax.ppermute(message_two, line, odd_pairs)  2.07 us
    all_to_all x1, waiting for transfers between devices, local(): lax.all_to_all(totals, near, 0, 0, axis_index_groups=turned(INNER_FIRST,...  1.87 us
  transfers between devices with their start and end apart: 6, of which 2 were waited for; matrix products, arithmetic and copies ran while one was open for 0% of the time, Pallas kernels for 8%

profile of v4, /device:TPU:1, one launch (start us, length us, event | category | flops | bytes accessed | tf_op | source)
XLA Modules:
  0.0 52.4 jit_solution(2523725513181853539)
XLA Ops:
  0.6 1.9 %totals.1 = f32[8,24,128]{2,1,0:T(8,128)} custom-call(f32[64,3072]{1,0:T(8,128)} %source.5, f32[1,64]{1,0:T(1,128)} %bitcast.11), custom_call_target="tpu_custom_call" | custom-call | bytes 786432 | tf_op jit(solution)/shard_map/totals/pallas_call | solution.py:420
  2.5 6.5 %all-to-all-start = ((f32[8,24,128]{2,1,0:T(8,128)}), f32[8,24,128]{2,1,0:T(8,128)S(1)}, u32[]{:S(2)}, u32[]{:S(2)}) async-start(f32[8,24,128]{2,1,0:T(8,128)} %totals.1), calls=%async_computation | async-start | bytes 196608 | tf_op jit(solution)/shard_map/all_to_all | solution.py:430
  9.0 3.1 %send.1 = (f32[8,4224]{1,0:T(8,128)S(1)}, f32[8,4224]{1,0:T(8,128)S(1)}, f32[64,3072]{1,0:T(8,128)S(1)}, f32[64,128]{1,0:T(8,128)S(1)}) custom-call(s32[1]{0:T(128)} %bitcast.2.kind, f32[3,64,3072]{2,1,0:T(8,128)} %fields.5, f32[64,3072]{1,0:T(8,128)} %source.5, f32[1,64]{1,0:T(1,128)} %bitcast.12, f32[4,64,128]{2,1,0:T(8,128)} %constant.43.clone.weights, ...), custom_call_target="tpu_custom_call" | custom-call | bytes 3145728 | tf_op jit(solution)/shard_map/send/pallas_call | solution.py:434
  12.1 1.9 %all-to-all-done.inner = f32[8,24,128]{2,1,0:T(8,128)S(1)} async-done(((f32[8,24,128]{2,1,0:T(8,128)}), f32[8,24,128]{2,1,0:T(8,128)S(1)}, u32[]{:S(2)}, u32[]{:S(2)}) %all-to-all-start) | async-done | bytes 98336 | tf_op jit(solution)/shard_map/all_to_all | solution.py:430
  14.0 0.7 %slab.1 = f32[8,24,128]{2,1,0:T(8,128)} custom-call(f32[8,24,128]{2,1,0:T(8,128)S(1)} %all-to-all-done.inner, f32[8,4224]{1,0:T(8,128)S(1)} %get-tuple-element.18.after_one, f32[8,4224]{1,0:T(8,128)S(1)} %get-tuple-element.19.after_two), custom_call_target="tpu_custom_call" | custom-call | tf_op jit(solution)/shard_map/slab/pallas_call | solution.py:452
  14.7 9.5 %all-to-all-start.1 = ((f32[8,24,128]{2,1,0:T(8,128)}), f32[8,24,128]{2,1,0:T(8,128)S(1)}, u32[]{:S(2)}, u32[]{:S(2)}) async-start(f32[8,24,128]{2,1,0:T(8,128)} %slab.1), calls=%async_computation.1 | async-start | bytes 196608 | tf_op jit(solution)/shard_map/all_to_all | solution.py:460
  24.1 1.1 %collective-permute-start = (f32[8,4224]{1,0:T(8,128)S(1)}, f32[8,4224]{1,0:T(8,128)S(1)}, u32[]{:S(2)}, u32[]{:S(2)}) collective-permute-start(f32[8,4224]{1,0:T(8,128)S(1)} %get-tuple-element.18.after_one), channel_id=1, source_target_pairs={{0,4},{4,0},{8,12},{12,8},{16,20},{20,16},{24,28},{28,24},{32,36},... | collective-permute-start | bytes 405512 | tf_op jit(solution)/shard_map/ppermute | solution.py:465
  25.2 2.1 %collective-permute-start.1 = (f32[8,4224]{1,0:T(8,128)S(1)}, f32[8,4224]{1,0:T(8,128)S(1)}, u32[]{:S(2)}, u32[]{:S(2)}) collective-permute-start(f32[8,4224]{1,0:T(8,128)S(1)} %get-tuple-element.19.after_two), channel_id=1, source_target_pairs={{4,8},{8,4},{12,16},{16,12},{20,24},{24,20},{28,32},{32,28},{36,40... | collective-permute-start | bytes 405512 | tf_op jit(solution)/shard_map/ppermute | solution.py:464
  27.3 0.0 all-to-all-done.1.outer
  27.3 0.9 %velocity.1 = (f32[64,3072]{1,0:T(8,128)S(1)}, f32[1,3072]{1,0:T(1,128)S(1)}, f32[128,128]{1,0:T(8,128)}) custom-call(s32[1]{0:T(128)} %bitcast.place, s32[1]{0:T(128)} %bitcast.1.slab, f32[64,3072]{1,0:T(8,128)S(1)} %get-tuple-element.16.running, f32[64,128]{1,0:T(8,128)S(1)} %get-tuple-element.17.spread, f32[8,24,128]{2,1,0:T(8,128)S(1)} %all-to-all-done.inner, ...), custom_call_target="tpu_custom_call" | custom-call | bytes 1572864 | tf_op jit(solution)/shard_map/velocity/pallas_call | solution.py:467
  28.3 14.7 %all-to-all-start.2 = ((f32[128,1,128]{2,1,0:T(1,128)}), f32[128,1,128]{2,1,0:T(1,128)S(1)}, u32[]{:S(2)}, u32[]{:S(2)}) async-start(f32[128,1,128]{2,1,0:T(1,128)} %bitcast.5), calls=%async_computation.2 | async-start | bytes 131072 | tf_op jit(solution)/shard_map/all_to_all | solution.py:479
  43.0 0.0 collective-permute-done.message_one
  43.0 0.0 collective-permute-done.1.message_two
  43.0 3.4 %tendency.1 = (f32[3,64,3072]{2,1,0:T(8,128)S(1)}, f32[64,3072]{1,0:T(8,128)}) custom-call(s32[1]{0:T(128)} %bitcast.2.kind, f32[3,64,3072]{2,1,0:T(8,128)} %fields.5, f32[64,3072]{1,0:T(8,128)} %source.5, f32[64,3072]{1,0:T(8,128)S(1)} %get-tuple-element.21.velocity, f32[1,3072]{1,0:T(1,128)S(1)} %get-tuple-element.22.offset, ...), custom_call_target="tpu_custom_call" | custom-call | bytes 9437184 | tf_op jit(solution)/shard_map/tendency/pallas_call | solution.py:481
  46.5 0.0 all-to-all-done.2
  46.5 1.4 %collective-permute-start.2 = (f32[128,128]{1,0:T(8,128)S(1)}, f32[128,128]{1,0:T(8,128)S(1)}, u32[]{:S(2)}, u32[]{:S(2)}) collective-permute-start(f32[128,128]{1,0:T(8,128)S(1)} %bitcast.9), channel_id=1, source_target_pairs={{0,4},{4,0},{1,5},{5,1},{2,6},{6,2},{3,7},{7,3},{8,12},{12,8},{9,1... | collective-permute-start | bytes 196616 | tf_op jit(solution)/shard_map/ppermute | solution.py:505
  47.9 0.9 %collective-permute-done.2.more_rates = f32[128,128]{1,0:T(8,128)S(1)} collective-permute-done((f32[128,128]{1,0:T(8,128)S(1)}, f32[128,128]{1,0:T(8,128)S(1)}, u32[]{:S(2)}, u32[]{:S(2)}) %collective-permute-start.2) | collective-permute-done | bytes 65568 | tf_op jit(solution)/shard_map/ppermute | solution.py:505
  48.8 3.6 %update.1 = (f32[3,64,3072]{2,1,0:T(8,128)}, f32[3,64,3072]{2,1,0:T(8,128)}) custom-call(f32[3,64,3072]{2,1,0:T(8,128)} %fields.5, f32[3,64,3072]{2,1,0:T(8,128)} %register.1, f32[3,64,3072]{2,1,0:T(8,128)S(1)} %get-tuple-element.24.tendency, f32[128,128]{1,0:T(8,128)S(1)} %bitcast.10, f32[128,128]{1,0:T(8,128)S(1)} %collective-permute-done.2.more_rates), custom_call_target="tpu_custom_call" | custom-call | bytes 9437184 | tf_op jit(solution)/shard_map/update/pallas_call | solution.py:506
Async XLA Ops:
  2.5 11.5 %all-to-all-start = ((f32[8,24,128]{2,1,0:T(8,128)}), f32[8,24,128]{2,1,0:T(8,128)S(1)}, u32[]{:S(2)}, u32[]{:S(2)}) async-start(f32[8,24,128]{2,1,0:T(8,128)} %totals.1), calls=%async_computation | async-start | bytes 196608 | tf_op jit(solution)/shard_map/all_to_all | solution.py:430
  14.7 12.7 %all-to-all-start.1 = ((f32[8,24,128]{2,1,0:T(8,128)}), f32[8,24,128]{2,1,0:T(8,128)S(1)}, u32[]{:S(2)}, u32[]{:S(2)}) async-start(f32[8,24,128]{2,1,0:T(8,128)} %slab.1), calls=%async_computation.1 | async-start | bytes 196608 | tf_op jit(solution)/shard_map/all_to_all | solution.py:460
  24.1 18.9 %collective-permute-start = (f32[8,4224]{1,0:T(8,128)S(1)}, f32[8,4224]{1,0:T(8,128)S(1)}, u32[]{:S(2)}, u32[]{:S(2)}) collective-permute-start(f32[8,4224]{1,0:T(8,128)S(1)} %get-tuple-element.18.after_one), channel_id=1, source_target_pairs={{0,4},{4,0},{8,12},{12,8},{16,20},{20,16},{24,28},{28,24},{32,36},... | collective-permute-start | bytes 405512 | tf_op jit(solution)/shard_map/ppermute | solution.py:465
  25.2 17.8 %collective-permute-start.1 = (f32[8,4224]{1,0:T(8,128)S(1)}, f32[8,4224]{1,0:T(8,128)S(1)}, u32[]{:S(2)}, u32[]{:S(2)}) collective-permute-start(f32[8,4224]{1,0:T(8,128)S(1)} %get-tuple-element.19.after_two), channel_id=1, source_target_pairs={{4,8},{8,4},{12,16},{16,12},{20,24},{24,20},{28,32},{32,28},{36,40... | collective-permute-start | bytes 405512 | tf_op jit(solution)/shard_map/ppermute | solution.py:464
  28.3 18.2 %all-to-all-start.2 = ((f32[128,1,128]{2,1,0:T(1,128)}), f32[128,1,128]{2,1,0:T(1,128)S(1)}, u32[]{:S(2)}, u32[]{:S(2)}) async-start(f32[128,1,128]{2,1,0:T(1,128)} %bitcast.5), calls=%async_computation.2 | async-start | bytes 131072 | tf_op jit(solution)/shard_map/all_to_all | solution.py:479
  46.5 2.3 %collective-permute-start.2 = (f32[128,128]{1,0:T(8,128)S(1)}, f32[128,128]{1,0:T(8,128)S(1)}, u32[]{:S(2)}, u32[]{:S(2)}) collective-permute-start(f32[128,128]{1,0:T(8,128)S(1)} %bitcast.9), channel_id=1, source_target_pairs={{0,4},{4,0},{1,5},{5,1},{2,6},{6,2},{3,7},{7,3},{8,12},{12,8},{9,1... | collective-permute-start | bytes 196616 | tf_op jit(solution)/shard_map/ppermute | solution.py:505

commit v5 on v4

--- a/solution.py
+++ b/solution.py
@@ -24,7 +24,7 @@
 LANES = 128
 SLAB_FIRST = 4
 INNER_FIRST = 0
-RATE_FIRST = (4, 2, 2)
+RATE_FIRST = (4, 1, 2)
 STEPS = 4
 GRANT = 24 * 1024 * 1024
 MESSAGE = 11

time: 52.8 us -> 52.5 us (level)
    all_to_all x1, starting transfers between devices: 14.7 us -> 14.2 us  [local(): lax.all_to_all(rate, same_core, 0, 0, axis_index_groups=[order], tiled=True)]
where the time goes in v5:
time: 52.5 us; the launch traced here: 52.1 us
  starting transfers between devices  35 us (67%)
  Pallas kernels  13.6 us (26%)
  waiting for transfers between devices  2.8 us (5%)
  between operations  0.7 us (1%)
    all_to_all x1, starting transfers between devices, local(): lax.all_to_all(rate, same_core, 0, 0, axis_index_groups=[order], tiled=True)  14.2 us
    all_to_all x1, starting transfers between devices, local(): lax.all_to_all(slab_sums, 'slab', 0, 0, axis_index_groups=turned(SLAB_FIR...  9.47 us
    all_to_all x1, starting transfers between devices, local(): lax.all_to_all(totals, near, 0, 0, axis_index_groups=turned(INNER_FIRST,...  6.52 us
    pallas_call x1, Pallas kernels, local(): pl.pallas_call(update_kernel, in_specs=[hbm, hbm, vmem, vmem, vmem], out_...  3.59 us
    pallas_call x1, Pallas kernels, local(): pl.pallas_call(tendency_kernel, in_specs=[smem, hbm, hbm, vmem, vmem, vme...  3.44 us
    pallas_call x1, Pallas kernels, local(): pl.pallas_call(send_kernel, in_specs=[smem, hbm, hbm, hbm, hbm, hbm], out...  3.13 us
    ppermute x1, starting transfers between devices, local(): got_two = lax.ppermute(message_two, line, odd_pairs)  2.07 us
    all_to_all x1, waiting for transfers between devices, local(): lax.all_to_all(totals, near, 0, 0, axis_index_groups=turned(INNER_FIRST,...  1.87 us
  transfers between devices with their start and end apart: 6, of which 2 were waited for; matrix products, arithmetic and copies ran while one was open for 0% of the time, Pallas kernels for 8%

profile of v5, /device:TPU:1, one launch (start us, length us, event | category | flops | bytes accessed | tf_op | source)
XLA Modules:
  0.0 52.1 jit_solution(7867550832290474436)
XLA Ops:
  0.6 1.9 %totals.1 = f32[8,24,128]{2,1,0:T(8,128)} custom-call(f32[64,3072]{1,0:T(8,128)} %source.5, f32[1,64]{1,0:T(1,128)} %bitcast.11), custom_call_target="tpu_custom_call" | custom-call | bytes 786432 | tf_op jit(solution)/shard_map/totals/pallas_call | solution.py:420
  2.5 6.5 %all-to-all-start = ((f32[8,24,128]{2,1,0:T(8,128)}), f32[8,24,128]{2,1,0:T(8,128)S(1)}, u32[]{:S(2)}, u32[]{:S(2)}) async-start(f32[8,24,128]{2,1,0:T(8,128)} %totals.1), calls=%async_computation | async-start | bytes 196608 | tf_op jit(solution)/shard_map/all_to_all | solution.py:430
  9.0 3.1 %send.1 = (f32[8,4224]{1,0:T(8,128)S(1)}, f32[8,4224]{1,0:T(8,128)S(1)}, f32[64,3072]{1,0:T(8,128)S(1)}, f32[64,128]{1,0:T(8,128)S(1)}) custom-call(s32[1]{0:T(128)} %bitcast.2.kind, f32[3,64,3072]{2,1,0:T(8,128)} %fields.5, f32[64,3072]{1,0:T(8,128)} %source.5, f32[1,64]{1,0:T(1,128)} %bitcast.12, f32[4,64,128]{2,1,0:T(8,128)} %constant.43.clone.weights, ...), custom_call_target="tpu_custom_call" | custom-call | bytes 3145728 | tf_op jit(solution)/shard_map/send/pallas_call | solution.py:434
  12.1 1.9 %all-to-all-done.inner = f32[8,24,128]{2,1,0:T(8,128)S(1)} async-done(((f32[8,24,128]{2,1,0:T(8,128)}), f32[8,24,128]{2,1,0:T(8,128)S(1)}, u32[]{:S(2)}, u32[]{:S(2)}) %all-to-all-start) | async-done | bytes 98336 | tf_op jit(solution)/shard_map/all_to_all | solution.py:430
  14.0 0.7 %slab.1 = f32[8,24,128]{2,1,0:T(8,128)} custom-call(f32[8,24,128]{2,1,0:T(8,128)S(1)} %all-to-all-done.inner, f32[8,4224]{1,0:T(8,128)S(1)} %get-tuple-element.18.after_one, f32[8,4224]{1,0:T(8,128)S(1)} %get-tuple-element.19.after_two), custom_call_target="tpu_custom_call" | custom-call | tf_op jit(solution)/shard_map/slab/pallas_call | solution.py:452
  14.7 9.5 %all-to-all-start.1 = ((f32[8,24,128]{2,1,0:T(8,128)}), f32[8,24,128]{2,1,0:T(8,128)S(1)}, u32[]{:S(2)}, u32[]{:S(2)}) async-start(f32[8,24,128]{2,1,0:T(8,128)} %slab.1), calls=%async_computation.1 | async-start | bytes 196608 | tf_op jit(solution)/shard_map/all_to_all | solution.py:460
  24.1 1.1 %collective-permute-start = (f32[8,4224]{1,0:T(8,128)S(1)}, f32[8,4224]{1,0:T(8,128)S(1)}, u32[]{:S(2)}, u32[]{:S(2)}) collective-permute-start(f32[8,4224]{1,0:T(8,128)S(1)} %get-tuple-element.18.after_one), channel_id=1, source_target_pairs={{0,4},{4,0},{8,12},{12,8},{16,20},{20,16},{24,28},{28,24},{32,36},... | collective-permute-start | bytes 405512 | tf_op jit(solution)/shard_map/ppermute | solution.py:465
  25.2 2.1 %collective-permute-start.1 = (f32[8,4224]{1,0:T(8,128)S(1)}, f32[8,4224]{1,0:T(8,128)S(1)}, u32[]{:S(2)}, u32[]{:S(2)}) collective-permute-start(f32[8,4224]{1,0:T(8,128)S(1)} %get-tuple-element.19.after_two), channel_id=1, source_target_pairs={{4,8},{8,4},{12,16},{16,12},{20,24},{24,20},{28,32},{32,28},{36,40... | collective-permute-start | bytes 405512 | tf_op jit(solution)/shard_map/ppermute | solution.py:464
  27.3 0.0 all-to-all-done.1.outer
  27.3 0.9 %velocity.1 = (f32[64,3072]{1,0:T(8,128)S(1)}, f32[1,3072]{1,0:T(1,128)S(1)}, f32[128,128]{1,0:T(8,128)}) custom-call(s32[1]{0:T(128)} %bitcast.place, s32[1]{0:T(128)} %bitcast.1.slab, f32[64,3072]{1,0:T(8,128)S(1)} %get-tuple-element.16.running, f32[64,128]{1,0:T(8,128)S(1)} %get-tuple-element.17.spread, f32[8,24,128]{2,1,0:T(8,128)S(1)} %all-to-all-done.inner, ...), custom_call_target="tpu_custom_call" | custom-call | bytes 1572864 | tf_op jit(solution)/shard_map/velocity/pallas_call | solution.py:467
  28.3 14.2 %all-to-all-start.2 = ((f32[128,1,128]{2,1,0:T(1,128)}), f32[128,1,128]{2,1,0:T(1,128)S(1)}, u32[]{:S(2)}, u32[]{:S(2)}) async-start(f32[128,1,128]{2,1,0:T(1,128)} %bitcast.5), calls=%async_computation.2 | async-start | bytes 131072 | tf_op jit(solution)/shard_map/all_to_all | solution.py:479
  42.4 0.0 collective-permute-done.message_one
  42.4 0.0 collective-permute-done.1.message_two
  42.5 3.4 %tendency.1 = (f32[3,64,3072]{2,1,0:T(8,128)S(1)}, f32[64,3072]{1,0:T(8,128)}) custom-call(s32[1]{0:T(128)} %bitcast.2.kind, f32[3,64,3072]{2,1,0:T(8,128)} %fields.5, f32[64,3072]{1,0:T(8,128)} %source.5, f32[64,3072]{1,0:T(8,128)S(1)} %get-tuple-element.21.velocity, f32[1,3072]{1,0:T(1,128)S(1)} %get-tuple-element.22.offset, ...), custom_call_target="tpu_custom_call" | custom-call | bytes 9437184 | tf_op jit(solution)/shard_map/tendency/pallas_call | solution.py:481
  45.9 0.0 all-to-all-done.2
  45.9 1.6 %collective-permute-start.2 = (f32[128,128]{1,0:T(8,128)S(1)}, f32[128,128]{1,0:T(8,128)S(1)}, u32[]{:S(2)}, u32[]{:S(2)}) collective-permute-start(f32[128,128]{1,0:T(8,128)S(1)} %bitcast.9), channel_id=1, source_target_pairs={{0,4},{4,0},{1,5},{5,1},{2,6},{6,2},{3,7},{7,3},{8,12},{12,8},{9,1... | collective-permute-start | bytes 196616 | tf_op jit(solution)/shard_map/ppermute | solution.py:505
  47.6 0.9 %collective-permute-done.2.more_rates = f32[128,128]{1,0:T(8,128)S(1)} collective-permute-done((f32[128,128]{1,0:T(8,128)S(1)}, f32[128,128]{1,0:T(8,128)S(1)}, u32[]{:S(2)}, u32[]{:S(2)}) %collective-permute-start.2) | collective-permute-done | bytes 65568 | tf_op jit(solution)/shard_map/ppermute | solution.py:505
  48.5 3.6 %update.1 = (f32[3,64,3072]{2,1,0:T(8,128)}, f32[3,64,3072]{2,1,0:T(8,128)}) custom-call(f32[3,64,3072]{2,1,0:T(8,128)} %fields.5, f32[3,64,3072]{2,1,0:T(8,128)} %register.1, f32[3,64,3072]{2,1,0:T(8,128)S(1)} %get-tuple-element.24.tendency, f32[128,128]{1,0:T(8,128)S(1)} %bitcast.10, f32[128,128]{1,0:T(8,128)S(1)} %collective-permute-done.2.more_rates), custom_call_target="tpu_custom_call" | custom-call | bytes 9437184 | tf_op jit(solution)/shard_map/update/pallas_call | solution.py:506
Async XLA Ops:
  2.5 11.5 %all-to-all-start = ((f32[8,24,128]{2,1,0:T(8,128)}), f32[8,24,128]{2,1,0:T(8,128)S(1)}, u32[]{:S(2)}, u32[]{:S(2)}) async-start(f32[8,24,128]{2,1,0:T(8,128)} %totals.1), calls=%async_computation | async-start | bytes 196608 | tf_op jit(solution)/shard_map/all_to_all | solution.py:430
  14.7 12.7 %all-to-all-start.1 = ((f32[8,24,128]{2,1,0:T(8,128)}), f32[8,24,128]{2,1,0:T(8,128)S(1)}, u32[]{:S(2)}, u32[]{:S(2)}) async-start(f32[8,24,128]{2,1,0:T(8,128)} %slab.1), calls=%async_computation.1 | async-start | bytes 196608 | tf_op jit(solution)/shard_map/all_to_all | solution.py:460
  24.1 18.3 %collective-permute-start = (f32[8,4224]{1,0:T(8,128)S(1)}, f32[8,4224]{1,0:T(8,128)S(1)}, u32[]{:S(2)}, u32[]{:S(2)}) collective-permute-start(f32[8,4224]{1,0:T(8,128)S(1)} %get-tuple-element.18.after_one), channel_id=1, source_target_pairs={{0,4},{4,0},{8,12},{12,8},{16,20},{20,16},{24,28},{28,24},{32,36},... | collective-permute-start | bytes 405512 | tf_op jit(solution)/shard_map/ppermute | solution.py:465
  25.2 17.2 %collective-permute-start.1 = (f32[8,4224]{1,0:T(8,128)S(1)}, f32[8,4224]{1,0:T(8,128)S(1)}, u32[]{:S(2)}, u32[]{:S(2)}) collective-permute-start(f32[8,4224]{1,0:T(8,128)S(1)} %get-tuple-element.19.after_two), channel_id=1, source_target_pairs={{4,8},{8,4},{12,16},{16,12},{20,24},{24,20},{28,32},{32,28},{36,40... | collective-permute-start | bytes 405512 | tf_op jit(solution)/shard_map/ppermute | solution.py:464
  28.3 17.7 %all-to-all-start.2 = ((f32[128,1,128]{2,1,0:T(1,128)}), f32[128,1,128]{2,1,0:T(1,128)S(1)}, u32[]{:S(2)}, u32[]{:S(2)}) async-start(f32[128,1,128]{2,1,0:T(1,128)} %bitcast.5), calls=%async_computation.2 | async-start | bytes 131072 | tf_op jit(solution)/shard_map/all_to_all | solution.py:479
  45.9 2.5 %collective-permute-start.2 = (f32[128,128]{1,0:T(8,128)S(1)}, f32[128,128]{1,0:T(8,128)S(1)}, u32[]{:S(2)}, u32[]{:S(2)}) collective-permute-start(f32[128,128]{1,0:T(8,128)S(1)} %bitcast.9), channel_id=1, source_target_pairs={{0,4},{4,0},{1,5},{5,1},{2,6},{6,2},{3,7},{7,3},{8,12},{12,8},{9,1... | collective-permute-start | bytes 196616 | tf_op jit(solution)/shard_map/ppermute | solution.py:505

commit v6 on v5

--- a/solution.py
+++ b/solution.py
@@ -22,6 +22,7 @@
 STEP_FACTOR = 15.0 / 16.0
 
 LANES = 128
+TILE = 256
 SLAB_FIRST = 4
 INNER_FIRST = 0
 RATE_FIRST = (4, 1, 2)
@@ -338,8 +339,14 @@
             field = held_fields[k, :, p]
             tail = tails((3 * k, 3 * k + 1, 3 * k + 2, None), i, None)
             weights = mixed if k < 2 else mixed_scalar
-            both = jnp.dot(weights[...], stacked(field, tail), preferred_element_type=jnp.float32)
-            tendency[k, :, p] = both[cells:] - (speed * both[:cells] + field * velocity_x)
+            right = stacked(field, tail)
+            for low in range(0, width, TILE):
+                here = slice(low, low + TILE)
+                both = jnp.dot(weights[...], right[:, here], preferred_element_type=jnp.float32)
+                there = slice(p.start + low, p.start + low + TILE)
+                tendency[k, :, there] = both[cells:] - (
+                    speed[:, here] * both[:cells] + field[:, here] * velocity_x[:, here]
+                )
     out_copy.wait()
 
 

time: 52.5 us -> 52.5 us (level)
  no operation moved by 1% of the time
where the time goes in v6:
time: 52.5 us; the launch traced here: 52.1 us
  starting transfers between devices  35 us (67%)
  Pallas kernels  13.6 us (26%)
  waiting for transfers between devices  2.8 us (5%)
  between operations  0.7 us (1%)
    all_to_all x1, starting transfers between devices, local(): lax.all_to_all(rate, same_core, 0, 0, axis_index_groups=[order], tiled=True)  14.2 us
    all_to_all x1, starting transfers between devices, local(): lax.all_to_all(slab_sums, 'slab', 0, 0, axis_index_groups=turned(SLAB_FIR...  9.47 us
    all_to_all x1, starting transfers between devices, local(): lax.all_to_all(totals, near, 0, 0, axis_index_groups=turned(INNER_FIRST,...  6.52 us
    pallas_call x1, Pallas kernels, local(): pl.pallas_call(update_kernel, in_specs=[hbm, hbm, vmem, vmem, vmem], out_...  3.59 us
    pallas_call x1, Pallas kernels, local(): pl.pallas_call(tendency_kernel, in_specs=[smem, hbm, hbm, vmem, vmem, vme...  3.44 us
    pallas_call x1, Pallas kernels, local(): pl.pallas_call(send_kernel, in_specs=[smem, hbm, hbm, hbm, hbm, hbm], out...  3.13 us
    ppermute x1, starting transfers between devices, local(): got_two = lax.ppermute(message_two, line, odd_pairs)  2.07 us
    all_to_all x1, waiting for transfers between devices, local(): lax.all_to_all(totals, near, 0, 0, axis_index_groups=turned(INNER_FIRST,...  1.87 us
  transfers between devices with their start and end apart: 6, of which 2 were waited for; matrix products, arithmetic and copies ran while one was open for 0% of the time, Pallas kernels for 8%

profile of v6, /device:TPU:1, one launch (start us, length us, event | category | flops | bytes accessed | tf_op | source)
XLA Modules:
  0.0 52.1 jit_solution(7867550832290474436)
XLA Ops:
  0.6 1.9 %totals.1 = f32[8,24,128]{2,1,0:T(8,128)} custom-call(f32[64,3072]{1,0:T(8,128)} %source.5, f32[1,64]{1,0:T(1,128)} %bitcast.11), custom_call_target="tpu_custom_call" | custom-call | bytes 786432 | tf_op jit(solution)/shard_map/totals/pallas_call | solution.py:427
  2.5 6.5 %all-to-all-start = ((f32[8,24,128]{2,1,0:T(8,128)}), f32[8,24,128]{2,1,0:T(8,128)S(1)}, u32[]{:S(2)}, u32[]{:S(2)}) async-start(f32[8,24,128]{2,1,0:T(8,128)} %totals.1), calls=%async_computation | async-start | bytes 196608 | tf_op jit(solution)/shard_map/all_to_all | solution.py:437
  9.0 3.1 %send.1 = (f32[8,4224]{1,0:T(8,128)S(1)}, f32[8,4224]{1,0:T(8,128)S(1)}, f32[64,3072]{1,0:T(8,128)S(1)}, f32[64,128]{1,0:T(8,128)S(1)}) custom-call(s32[1]{0:T(128)} %bitcast.2.kind, f32[3,64,3072]{2,1,0:T(8,128)} %fields.5, f32[64,3072]{1,0:T(8,128)} %source.5, f32[1,64]{1,0:T(1,128)} %bitcast.12, f32[4,64,128]{2,1,0:T(8,128)} %constant.43.clone.weights, ...), custom_call_target="tpu_custom_call" | custom-call | bytes 3145728 | tf_op jit(solution)/shard_map/send/pallas_call | solution.py:441
  12.1 1.9 %all-to-all-done.inner = f32[8,24,128]{2,1,0:T(8,128)S(1)} async-done(((f32[8,24,128]{2,1,0:T(8,128)}), f32[8,24,128]{2,1,0:T(8,128)S(1)}, u32[]{:S(2)}, u32[]{:S(2)}) %all-to-all-start) | async-done | bytes 98336 | tf_op jit(solution)/shard_map/all_to_all | solution.py:437
  14.0 0.7 %slab.1 = f32[8,24,128]{2,1,0:T(8,128)} custom-call(f32[8,24,128]{2,1,0:T(8,128)S(1)} %all-to-all-done.inner, f32[8,4224]{1,0:T(8,128)S(1)} %get-tuple-element.18.after_one, f32[8,4224]{1,0:T(8,128)S(1)} %get-tuple-element.19.after_two), custom_call_target="tpu_custom_call" | custom-call | tf_op jit(solution)/shard_map/slab/pallas_call | solution.py:459
  14.7 9.5 %all-to-all-start.1 = ((f32[8,24,128]{2,1,0:T(8,128)}), f32[8,24,128]{2,1,0:T(8,128)S(1)}, u32[]{:S(2)}, u32[]{:S(2)}) async-start(f32[8,24,128]{2,1,0:T(8,128)} %slab.1), calls=%async_computation.1 | async-start | bytes 196608 | tf_op jit(solution)/shard_map/all_to_all | solution.py:467
  24.1 1.1 %collective-permute-start = (f32[8,4224]{1,0:T(8,128)S(1)}, f32[8,4224]{1,0:T(8,128)S(1)}, u32[]{:S(2)}, u32[]{:S(2)}) collective-permute-start(f32[8,4224]{1,0:T(8,128)S(1)} %get-tuple-element.18.after_one), channel_id=1, source_target_pairs={{0,4},{4,0},{8,12},{12,8},{16,20},{20,16},{24,28},{28,24},{32,36},... | collective-permute-start | bytes 405512 | tf_op jit(solution)/shard_map/ppermute | solution.py:472
  25.2 2.1 %collective-permute-start.1 = (f32[8,4224]{1,0:T(8,128)S(1)}, f32[8,4224]{1,0:T(8,128)S(1)}, u32[]{:S(2)}, u32[]{:S(2)}) collective-permute-start(f32[8,4224]{1,0:T(8,128)S(1)} %get-tuple-element.19.after_two), channel_id=1, source_target_pairs={{4,8},{8,4},{12,16},{16,12},{20,24},{24,20},{28,32},{32,28},{36,40... | collective-permute-start | bytes 405512 | tf_op jit(solution)/shard_map/ppermute | solution.py:471
  27.3 0.0 all-to-all-done.1.outer
  27.3 0.9 %velocity.1 = (f32[64,3072]{1,0:T(8,128)S(1)}, f32[1,3072]{1,0:T(1,128)S(1)}, f32[128,128]{1,0:T(8,128)}) custom-call(s32[1]{0:T(128)} %bitcast.place, s32[1]{0:T(128)} %bitcast.1.slab, f32[64,3072]{1,0:T(8,128)S(1)} %get-tuple-element.16.running, f32[64,128]{1,0:T(8,128)S(1)} %get-tuple-element.17.spread, f32[8,24,128]{2,1,0:T(8,128)S(1)} %all-to-all-done.inner, ...), custom_call_target="tpu_custom_call" | custom-call | bytes 1572864 | tf_op jit(solution)/shard_map/velocity/pallas_call | solution.py:474
  28.3 14.2 %all-to-all-start.2 = ((f32[128,1,128]{2,1,0:T(1,128)}), f32[128,1,128]{2,1,0:T(1,128)S(1)}, u32[]{:S(2)}, u32[]{:S(2)}) async-start(f32[128,1,128]{2,1,0:T(1,128)} %bitcast.5), calls=%async_computation.2 | async-start | bytes 131072 | tf_op jit(solution)/shard_map/all_to_all | solution.py:486
  42.4 0.0 collective-permute-done.message_one
  42.4 0.0 collective-permute-done.1.message_two
  42.5 3.4 %tendency.1 = (f32[3,64,3072]{2,1,0:T(8,128)S(1)}, f32[64,3072]{1,0:T(8,128)}) custom-call(s32[1]{0:T(128)} %bitcast.2.kind, f32[3,64,3072]{2,1,0:T(8,128)} %fields.5, f32[64,3072]{1,0:T(8,128)} %source.5, f32[64,3072]{1,0:T(8,128)S(1)} %get-tuple-element.21.velocity, f32[1,3072]{1,0:T(1,128)S(1)} %get-tuple-element.22.offset, ...), custom_call_target="tpu_custom_call" | custom-call | bytes 9437184 | tf_op jit(solution)/shard_map/tendency/pallas_call | solution.py:488
  45.9 0.0 all-to-all-done.2
  45.9 1.6 %collective-permute-start.2 = (f32[128,128]{1,0:T(8,128)S(1)}, f32[128,128]{1,0:T(8,128)S(1)}, u32[]{:S(2)}, u32[]{:S(2)}) collective-permute-start(f32[128,128]{1,0:T(8,128)S(1)} %bitcast.9), channel_id=1, source_target_pairs={{0,4},{4,0},{1,5},{5,1},{2,6},{6,2},{3,7},{7,3},{8,12},{12,8},{9,1... | collective-permute-start | bytes 196616 | tf_op jit(solution)/shard_map/ppermute | solution.py:512
  47.6 0.9 %collective-permute-done.2.more_rates = f32[128,128]{1,0:T(8,128)S(1)} collective-permute-done((f32[128,128]{1,0:T(8,128)S(1)}, f32[128,128]{1,0:T(8,128)S(1)}, u32[]{:S(2)}, u32[]{:S(2)}) %collective-permute-start.2) | collective-permute-done | bytes 65568 | tf_op jit(solution)/shard_map/ppermute | solution.py:512
  48.5 3.6 %update.1 = (f32[3,64,3072]{2,1,0:T(8,128)}, f32[3,64,3072]{2,1,0:T(8,128)}) custom-call(f32[3,64,3072]{2,1,0:T(8,128)} %fields.5, f32[3,64,3072]{2,1,0:T(8,128)} %register.1, f32[3,64,3072]{2,1,0:T(8,128)S(1)} %get-tuple-element.24.tendency, f32[128,128]{1,0:T(8,128)S(1)} %bitcast.10, f32[128,128]{1,0:T(8,128)S(1)} %collective-permute-done.2.more_rates), custom_call_target="tpu_custom_call" | custom-call | bytes 9437184 | tf_op jit(solution)/shard_map/update/pallas_call | solution.py:513
Async XLA Ops:
  2.5 11.5 %all-to-all-start = ((f32[8,24,128]{2,1,0:T(8,128)}), f32[8,24,128]{2,1,0:T(8,128)S(1)}, u32[]{:S(2)}, u32[]{:S(2)}) async-start(f32[8,24,128]{2,1,0:T(8,128)} %totals.1), calls=%async_computation | async-start | bytes 196608 | tf_op jit(solution)/shard_map/all_to_all | solution.py:437
  14.7 12.7 %all-to-all-start.1 = ((f32[8,24,128]{2,1,0:T(8,128)}), f32[8,24,128]{2,1,0:T(8,128)S(1)}, u32[]{:S(2)}, u32[]{:S(2)}) async-start(f32[8,24,128]{2,1,0:T(8,128)} %slab.1), calls=%async_computation.1 | async-start | bytes 196608 | tf_op jit(solution)/shard_map/all_to_all | solution.py:467
  24.1 18.3 %collective-permute-start = (f32[8,4224]{1,0:T(8,128)S(1)}, f32[8,4224]{1,0:T(8,128)S(1)}, u32[]{:S(2)}, u32[]{:S(2)}) collective-permute-start(f32[8,4224]{1,0:T(8,128)S(1)} %get-tuple-element.18.after_one), channel_id=1, source_target_pairs={{0,4},{4,0},{8,12},{12,8},{16,20},{20,16},{24,28},{28,24},{32,36},... | collective-permute-start | bytes 405512 | tf_op jit(solution)/shard_map/ppermute | solution.py:472
  25.2 17.2 %collective-permute-start.1 = (f32[8,4224]{1,0:T(8,128)S(1)}, f32[8,4224]{1,0:T(8,128)S(1)}, u32[]{:S(2)}, u32[]{:S(2)}) collective-permute-start(f32[8,4224]{1,0:T(8,128)S(1)} %get-tuple-element.19.after_two), channel_id=1, source_target_pairs={{4,8},{8,4},{12,16},{16,12},{20,24},{24,20},{28,32},{32,28},{36,40... | collective-permute-start | bytes 405512 | tf_op jit(solution)/shard_map/ppermute | solution.py:471
  28.3 17.7 %all-to-all-start.2 = ((f32[128,1,128]{2,1,0:T(1,128)}), f32[128,1,128]{2,1,0:T(1,128)S(1)}, u32[]{:S(2)}, u32[]{:S(2)}) async-start(f32[128,1,128]{2,1,0:T(1,128)} %bitcast.5), calls=%async_computation.2 | async-start | bytes 131072 | tf_op jit(solution)/shard_map/all_to_all | solution.py:486
  45.9 2.5 %collective-permute-start.2 = (f32[128,128]{1,0:T(8,128)S(1)}, f32[128,128]{1,0:T(8,128)S(1)}, u32[]{:S(2)}, u32[]{:S(2)}) collective-permute-start(f32[128,128]{1,0:T(8,128)S(1)} %bitcast.9), channel_id=1, source_target_pairs={{0,4},{4,0},{1,5},{5,1},{2,6},{6,2},{3,7},{7,3},{8,12},{12,8},{9,1... | collective-permute-start | bytes 196616 | tf_op jit(solution)/shard_map/ppermute | solution.py:512
